TPU v7x, 128 devices: a whole 4x4x4 slice. The times are simulated.
128 devices in a mesh: dp: 8 (over x, core), fsdp: 16 (over z, y).
Axes of the slice: x: 4, y: 4, z: 4, core: 2. Of those that a mesh axis runs over, the one named last changes fastest.
Arguments:
- token_ids: int32 [48, 2048], P('dp', 'fsdp'), may hold values from 0 to 30521
- splits: int32 [48], P('dp'), may hold values from 512 to 1535
- valid_mask: int32 [48, 2048], P('dp', 'fsdp'), may hold values from 0 to 1, as said below
- embed_table: bfloat16 [30522, 128], replicated, may hold values from -6 to 6
- embed_proj: bfloat16 [384, 512], replicated, may hold values from -0.3125 to 0.3125
- embed_bias: float32 [512], replicated, may hold values from -1.75 to 1.75
- type_table: float32 [2, 512], replicated, may hold values from -3 to 3
- teach_in: bfloat16 [512, 1024], replicated, may hold values from -0.25 to 0.25
- teach_qkv: bfloat16 [1024, 3072], replicated, may hold values from -0.1875 to 0.1875
- teach_att: bfloat16 [1024, 1024], replicated, may hold values from -2 to 2
- teach_up: bfloat16 [1024, 4096], replicated, may hold values from -0.1875 to 0.1875
- teach_down: bfloat16 [4096, 1024], replicated, may hold values from -0.09375 to 0.09375
- teach_out: bfloat16 [1024, 512], replicated, may hold values from -0.1875 to 0.1875
- teach_bias: float32 [10752], replicated, may hold values from -0.625 to 0.625
- teach_gain: float32 [2560], replicated, may hold values from 0.5 to 1.5
- teach_shift: float32 [2560], replicated, may hold values from -1.75 to 1.75
- matrices: float32 [720896], P(('dp', 'fsdp'))
- vectors: float32 [6016], P(('dp', 'fsdp'))
- matrix_first: float32 [720896], P(('dp', 'fsdp')), may hold values from -3.8146973e-05 to 3.8146973e-05
- matrix_second: float32 [720896], P(('dp', 'fsdp')), may hold values from 3.439206e-12 to 1.3756824e-11
- vector_first: float32 [6016], P(('dp', 'fsdp')), may hold values from -0.00015258789 to 0.00015258789
- vector_second: float32 [6016], P(('dp', 'fsdp')), may hold values from 5.5027295e-11 to 2.2010918e-10
Outputs:
- loss_sum: float32 [], replicated
- query_count: float32 [], replicated
- grad_norm: float32 [], replicated
- new_matrices: float32 [720896], P(('dp', 'fsdp'))
- new_matrix_first: float32 [720896], P(('dp', 'fsdp'))
- new_matrix_second: float32 [720896], P(('dp', 'fsdp'))
- new_vectors: float32 [6016], P(('dp', 'fsdp'))
- new_vector_first: float32 [6016], P(('dp', 'fsdp'))
- new_vector_second: float32 [6016], P(('dp', 'fsdp'))
Inputs may be any that keep to these rules, and one draw needn't show every extreme that they name: `valid_mask`: 1 marks a query whose loss counts. `splits`: first token of the second segment of a row.
All inputs are finite; a program needn't handle non-finite values.
Results may differ from a plain program's by a relative error of at most 0.0076.
The roundings to bfloat16 on the way count: a program that leaves them out, or rounds other values in their place, can miss the bound.
Values may be sent and summed in bfloat16 or wider, within the bound.
A program may use at most 320 MiB of HBM per device.

v0:
```python
import math

import jax
import jax.numpy as jnp
from jax import lax
from jax.sharding import PartitionSpec as P

D_E = 512
D_T = 1024
FF_T = 4096
D_S = 128
FF_S = 512
HEADS = 4
FFN_COUNT = 4
STEP = 5
HEAD_T = 256
HEAD_S = 32


CLIP_NORM = 0.05
BETA_ONE = 0.9
BETA_TWO = 0.999
LEARN_RATE = 0.3
WEIGHT_DECAY = 0.01
ADAM_EPS = 1e-06


def padded(shard, sides, width):
    for axis, dim in sides:
        peers, length = (lax.axis_size(axis), shard.shape[dim])
        up = [(i, (i + 1) % peers) for i in range(peers - 1)]
        down = [(j, i) for i, j in up]
        last = lax.slice_in_dim(shard, length - width, length, axis=dim)
        first = lax.slice_in_dim(shard, 0, width, axis=dim)
        before = lax.ppermute(last, axis, up)
        after = lax.ppermute(first, axis, down)
        shard = jnp.concatenate([before, shard, after], axis=dim)
    return shard


def mat_layouts():
    return [
        (D_E, D_S),
        (D_S, 3 * D_S),
        (D_S, D_S),
        (FFN_COUNT, D_S, FF_S),
        (FFN_COUNT, FF_S, D_S),
        (D_S, D_E),
    ]


def vec_layouts():
    return [
        (D_S,),
        (3 * D_S,),
        (D_S,),
        (D_S,),
        (D_S,),
        (FFN_COUNT, FF_S),
        (FFN_COUNT, D_S),
        (FFN_COUNT, D_S),
        (FFN_COUNT, D_S),
        (D_E,),
        (D_E,),
        (D_E,),
    ]


def split_flat(flat, layouts):
    pieces = []
    offset = 0
    for layout in layouts:
        amount = math.prod(layout)
        pieces.append(flat[offset : offset + amount].reshape(layout))
        offset += amount
    return pieces


def layer_norm(values, gain, shift):
    center = values - jnp.mean(values, -1, keepdims=True)
    spread = jnp.mean(center * center, -1, keepdims=True)
    return center * lax.rsqrt(spread + 1e-05) * gain + shift


def gelu_slope(values):
    return (
        0.5 * (1.0 + lax.erf(values * 0.7071067811865476))
        + values * jnp.exp(-0.5 * values * values) * 0.3989422804014327
    )


def to_low(values):
    return values.astype(jnp.bfloat16)


def matmul(left, right):
    return jnp.dot(left, right, preferred_element_type=jnp.float32)


def weight_grad(acts, grads):
    return jnp.einsum("rtn,rtm->nm", acts, grads, preferred_element_type=jnp.float32)


def back_dot(grads, weight):
    return jnp.einsum("rtm,nm->rtn", grads, weight, preferred_element_type=jnp.float32)


def bias_grad(grads):
    return jnp.sum(grads.astype(jnp.float32), (0, 1))


def tensor_members(shard_len, base):
    bounds = []
    total = 0
    for layout in mat_layouts():
        total += math.prod(layout)
        bounds.append(total)
    upper = jnp.array(bounds, jnp.int32)
    lower = jnp.array([0] + bounds[:-1], jnp.int32)
    places = base + jnp.arange(shard_len, dtype=jnp.int32)
    inside = (places[None, :] >= lower[:, None]) & (places[None, :] < upper[:, None])
    return inside.astype(jnp.float32)


def teacher_pairs(hidden_low, weight, bias):
    return to_low(matmul(hidden_low, weight[:, D_T:]) + bias[D_T:])


def attend(queries, pairs, scale):
    rows, tokens, width = queries.shape
    keys = pairs[..., :width].reshape(rows, pairs.shape[1], HEADS, -1)
    values = pairs[..., width:].reshape(rows, pairs.shape[1], HEADS, -1)
    scores = (
        jnp.einsum(
            "rqhd,rkhd->rhqk",
            queries.reshape(rows, tokens, HEADS, -1),
            keys,
            preferred_element_type=jnp.float32,
        )
        * scale
    )
    probs = jax.nn.softmax(scores, -1)
    probs_low = to_low(probs)
    mixed = jnp.einsum("rhqk,rkhd->rqhd", probs_low, values, preferred_element_type=jnp.float32)
    return (scores, probs, probs_low, to_low(mixed.reshape(rows, tokens, width)))


def adam_parts(grad, first, second, master, decay, factor):
    grad = grad * factor
    first = BETA_ONE * first + (1.0 - BETA_ONE) * grad
    second = BETA_TWO * second + (1.0 - BETA_TWO) * grad * grad
    ratio = (
        first / (1.0 - BETA_ONE**STEP) / (jnp.sqrt(second / (1.0 - BETA_TWO**STEP)) + ADAM_EPS)
        + decay * master
    )
    return (first, second, ratio)


def per_device(
    token_ids,
    splits,
    valid_mask,
    embed_table,
    embed_proj,
    embed_bias,
    type_table,
    teach_in,
    teach_qkv,
    teach_att,
    teach_up,
    teach_down,
    teach_out,
    teach_bias,
    teach_gain,
    teach_shift,
    matrices,
    vectors,
    matrix_first,
    matrix_second,
    vector_first,
    vector_second,
):
    whole_mats, whole_vecs = (
        lax.all_gather(matrices.astype(jnp.bfloat16), ("dp", "fsdp"), axis=0, tiled=True),
        lax.all_gather(vectors.astype(jnp.bfloat16), ("dp", "fsdp"), axis=0, tiled=True),
    )
    in_weight, qkv_weight, att_weight, up_weight, down_weight, out_weight = split_flat(
        whole_mats, mat_layouts()
    )
    (
        in_bias,
        qkv_bias,
        att_bias,
        att_gain,
        att_shift,
        up_bias,
        down_bias,
        ffn_gain,
        ffn_shift,
        out_bias,
        out_gain,
        out_shift,
    ) = split_flat(whole_vecs.astype(jnp.float32), vec_layouts())
    members = tensor_members(matrices.shape[0], lax.axis_index(("dp", "fsdp")) * matrices.shape[0])
    square_w = jnp.sum(members * (matrices * matrices)[None, :], 1)
    count_local = jnp.sum(valid_mask.astype(jnp.float32))
    query_count = lax.psum(count_local, ("dp", "fsdp"))
    rows, tokens = token_ids.shape
    seq_len = tokens * lax.axis_size("fsdp")
    places = lax.axis_index("fsdp") * tokens + jnp.arange(tokens, dtype=jnp.int32)
    rimmed = padded(token_ids, (("fsdp", 1),), 1)
    left = jnp.where((places > 0)[None, :, None], embed_table[rimmed[:, :-2]], 0)
    right = jnp.where((places < seq_len - 1)[None, :, None], embed_table[rimmed[:, 2:]], 0)
    trigram = jnp.concatenate([left, embed_table[token_ids], right], -1)
    typed = jnp.where((places[None, :] >= splits[:, None])[..., None], type_table[1], type_table[0])
    embedded = to_low(matmul(trigram, embed_proj) + embed_bias + typed)
    source = embedded.astype(jnp.float32)
    teach_vecs = split_flat(teach_bias, [(D_T,), (3 * D_T,), (D_T,), (FF_T,), (D_T,), (D_E,)])
    gains = split_flat(teach_gain, [(D_T,), (D_T,), (D_E,)])
    shifts = split_flat(teach_shift, [(D_T,), (D_T,), (D_E,)])
    hidden = matmul(embedded, teach_in) + teach_vecs[0]
    hidden_low = to_low(hidden)
    t_query = to_low(matmul(hidden_low, teach_qkv[:, :D_T]) + teach_vecs[1][:D_T])
    t_own = teacher_pairs(hidden_low, teach_qkv, teach_vecs[1])
    first = matmul(embedded, in_weight) + in_bias
    s_qkv = to_low(matmul(to_low(first), qkv_weight) + qkv_bias)
    t_all, s_all = (
        lax.all_gather(t_own, "fsdp", axis=1, tiled=True),
        lax.all_gather(s_qkv[..., D_S:], "fsdp", axis=1, tiled=True),
    )
    t_scores, t_probs, t_probs_low, t_mixed = attend(t_query, t_all, HEAD_T ** (-0.5))
    normed = layer_norm(hidden + matmul(t_mixed, teach_att) + teach_vecs[2], gains[0], shifts[0])
    t_act = to_low(jax.nn.gelu(matmul(to_low(normed), teach_up) + teach_vecs[3], approximate=False))
    normed = layer_norm(normed + matmul(t_act, teach_down) + teach_vecs[4], gains[1], shifts[1])
    target = layer_norm(
        source + matmul(to_low(normed), teach_out) + teach_vecs[5], gains[2], shifts[2]
    )
    s_scores, s_probs, s_probs_low, s_mixed = attend(s_qkv[..., :D_S], s_all, HEAD_S ** (-0.5))
    branch = matmul(s_mixed, att_weight) + att_bias
    state = att_gain * (first + branch) + att_shift
    saved = []
    for index in range(FFN_COUNT):
        inner = matmul(to_low(state), up_weight[index]) + up_bias[index]
        act_low = to_low(jax.nn.gelu(inner, approximate=False))
        outer = matmul(act_low, down_weight[index]) + down_bias[index]
        saved.append((state, inner, act_low, outer))
        state = ffn_gain[index] * (state + outer) + ffn_shift[index]
    output = matmul(to_low(state), out_weight) + out_bias
    result = out_gain * (source + output) + out_shift
    diff = result - target
    t_lse = jax.nn.logsumexp(t_scores, -1)
    s_lse = jax.nn.logsumexp(s_scores, -1)
    kl_terms = jnp.sum(t_probs * (t_scores - s_scores), -1) - t_lse + s_lse
    weights = valid_mask.astype(jnp.float32)
    loss_local = jnp.sum(weights * (jnp.mean(kl_terms, 1) + jnp.mean(diff * diff, -1)))
    seed = weights / query_count
    d_result = (seed * (2.0 / D_E))[..., None] * diff
    grad_out_gain = jnp.sum(d_result * (source + output), (0, 1))
    grad_out_shift = jnp.sum(d_result, (0, 1))
    d_output = to_low(d_result * out_gain)
    grad_out_weight = weight_grad(to_low(state), d_output)
    grad_out_bias = bias_grad(d_output)
    d_state = back_dot(d_output, out_weight)
    ffn_grads = []
    for index in reversed(range(FFN_COUNT)):
        before, inner, act_low, outer = saved[index]
        gain_g = jnp.sum(d_state * (before + outer), (0, 1))
        shift_g = jnp.sum(d_state, (0, 1))
        d_sum = d_state * ffn_gain[index]
        d_outer = to_low(d_sum)
        down_g = weight_grad(act_low, d_outer)
        d_inner = to_low(back_dot(d_outer, down_weight[index]) * gelu_slope(inner))
        up_g = weight_grad(to_low(before), d_inner)
        ffn_grads.append((up_g, down_g, bias_grad(d_inner), bias_grad(d_outer), gain_g, shift_g))
        d_state = d_sum + back_dot(d_inner, up_weight[index])
    ffn_grads = ffn_grads[::-1]
    grad_att_gain = jnp.sum(d_state * (first + branch), (0, 1))
    grad_att_shift = jnp.sum(d_state, (0, 1))
    d_sum = d_state * att_gain
    d_branch = to_low(d_sum)
    grad_att_weight = weight_grad(s_mixed, d_branch)
    grad_att_bias = bias_grad(d_branch)
    d_mixed_flat = to_low(back_dot(d_branch, att_weight))
    d_mixed = d_mixed_flat.reshape(rows, tokens, HEADS, -1)
    keys = s_all[..., :D_S].reshape(rows, seq_len, HEADS, -1)
    values = s_all[..., D_S:].reshape(rows, seq_len, HEADS, -1)
    queries = s_qkv[..., :D_S].reshape(rows, tokens, HEADS, -1)
    d_probs = jnp.einsum("rqhd,rkhd->rhqk", d_mixed, values, preferred_element_type=jnp.float32)
    row_dot = jnp.sum(s_probs * d_probs, -1, keepdims=True)
    d_scores = s_probs * (d_probs - row_dot) + (seed / HEADS)[:, None, :, None] * (
        s_probs - t_probs
    )
    d_low = to_low(d_scores)
    scale = HEAD_S ** (-0.5)
    d_query = jnp.einsum("rhqk,rkhd->rqhd", d_low, keys, preferred_element_type=jnp.float32) * scale
    d_keys = (
        jnp.einsum("rhqk,rqhd->rkhd", d_low, queries, preferred_element_type=jnp.float32) * scale
    )
    d_values = jnp.einsum(
        "rhqk,rqhd->rkhd", s_probs_low, d_mixed, preferred_element_type=jnp.float32
    )
    own_keys, own_values = (
        lax.psum_scatter(
            d_keys.reshape(rows, seq_len, D_S).astype(jnp.bfloat16),
            "fsdp",
            scatter_dimension=1,
            tiled=True,
        ).astype(jnp.float32),
        lax.psum_scatter(
            d_values.reshape(rows, seq_len, D_S).astype(jnp.bfloat16),
            "fsdp",
            scatter_dimension=1,
            tiled=True,
        ).astype(jnp.float32),
    )
    d_qkv = to_low(jnp.concatenate([d_query.reshape(rows, tokens, D_S), own_keys, own_values], -1))
    grad_qkv_weight = weight_grad(to_low(first), d_qkv)
    d_first = to_low(d_sum + back_dot(d_qkv, qkv_weight))
    grad_in_weight = weight_grad(embedded, d_first)
    flat_mats = jnp.concatenate(
        [
            grad_in_weight.reshape(-1),
            grad_qkv_weight.reshape(-1),
            grad_att_weight.reshape(-1),
            jnp.stack([item[0] for item in ffn_grads]).reshape(-1),
            jnp.stack([item[1] for item in ffn_grads]).reshape(-1),
            grad_out_weight.reshape(-1),
        ]
    )
    flat_vecs = jnp.concatenate(
        [bias_grad(d_first), bias_grad(d_qkv), grad_att_bias, grad_att_gain, grad_att_shift]
        + [jnp.stack([item[slot] for item in ffn_grads]).reshape(-1) for slot in (2, 3, 4, 5)]
        + [grad_out_bias, grad_out_gain, grad_out_shift]
    )
    grad_mats, grad_vecs = (
        lax.psum_scatter(flat_mats, ("dp", "fsdp"), scatter_dimension=0, tiled=True),
        lax.psum_scatter(flat_vecs, ("dp", "fsdp"), scatter_dimension=0, tiled=True),
    )
    square_g = jnp.sum(grad_mats * grad_mats) + jnp.sum(grad_vecs * grad_vecs)
    loss_sum, grad_sq, weight_sq = lax.psum((loss_local, square_g, square_w), ("dp", "fsdp"))
    grad_norm = jnp.sqrt(grad_sq)
    factor = CLIP_NORM / jnp.maximum(grad_norm, CLIP_NORM)
    mat_first, mat_second, mat_ratio = adam_parts(
        grad_mats, matrix_first, matrix_second, matrices, WEIGHT_DECAY, factor
    )
    step_sq = lax.psum(jnp.sum(members * (mat_ratio * mat_ratio)[None, :], 1), ("dp", "fsdp"))
    trust = jnp.sqrt(weight_sq) / jnp.sqrt(step_sq)
    per_entry = jnp.sum(members * trust[:, None], 0)
    new_matrices = matrices - LEARN_RATE * (per_entry * mat_ratio)
    vec_first, vec_second, vec_ratio = adam_parts(
        grad_vecs, vector_first, vector_second, vectors, 0.0, factor
    )
    new_vectors = vectors - LEARN_RATE * vec_ratio
    return (
        loss_sum,
        query_count,
        grad_norm,
        new_matrices,
        mat_first,
        mat_second,
        new_vectors,
        vec_first,
        vec_second,
    )


def solution(mesh):
    return jax.shard_map(
        per_device,
        mesh=mesh,
        in_specs=(
            P("dp", "fsdp"),
            P("dp"),
            P("dp", "fsdp"),
            P(),
            P(),
            P(),
            P(),
            P(),
            P(),
            P(),
            P(),
            P(),
            P(),
            P(),
            P(),
            P(),
            P(("dp", "fsdp")),
            P(("dp", "fsdp")),
            P(("dp", "fsdp")),
            P(("dp", "fsdp")),
            P(("dp", "fsdp")),
            P(("dp", "fsdp")),
        ),
        out_specs=(
            P(),
            P(),
            P(),
            P(("dp", "fsdp")),
            P(("dp", "fsdp")),
            P(("dp", "fsdp")),
            P(("dp", "fsdp")),
            P(("dp", "fsdp")),
            P(("dp", "fsdp")),
        ),
        check_vma=False,
    )
```

profile of v0, /device:TPU:1, one launch (start us, length us, event | category | flops | bytes accessed | tf_op | source)
XLA Modules:
  0.0 1212.7 jit_solution(7835237941359153986)
XLA Ops:
  15.8 69.6 %all-reduce = bf16[6016]{0:T(1024)(128)(2,1)S(1)} all-reduce(bf16[6016]{0:T(1024)(128)(2,1)S(1)} %dynamic-update-slice), channel_id=1, replica_groups=mesh['dp'=8,'fsdp'=16] {'dp','fsdp'}, use_global_device_ids=true, to_apply=%add | all-reduce | flops 6016 | bytes 24064
  100.2 6.3 gather_fusion
  108.4 11.0 reduce
  133.2 7.2 add_convert_fusion.1
  141.6 64.3 %psum.36 = f32[]{:T(128)} all-reduce(f32[]{:T(128)} %convert_reduce_fusion.12), channel_id=1, replica_groups=mesh['dp'=8,'fsdp'=16] {'dp','fsdp'}, use_global_device_ids=true, to_apply=%region_18.19 | all-reduce | flops 1 | bytes 8 | tf_op jit(solution)/shard_map/psum | solution.py:207
  235.5 237.5 %all-gather.5.cloned.1.call-done = bf16[6,2048,2048]{2,1,0:T(8,128)(2,1)} async-done(((bf16[6,128,2048]{2,1,0:T(8,128)(2,1)}), bf16[6,2048,2048]{2,1,0:T(8,128)(2,1)}) %all-gather.5.cloned.1.call-update) | async-done | bytes 50331664 | tf_op jit(solution)/shard_map/all_gather | solution.py:228
  473.0 33.2 %fusion.253 = (bf16[6,2048,1024]{2,1,0:T(8,128)(2,1)}, bf16[6,2048,1024]{2,1,0:T(8,128)(2,1)}) fusion(bf16[6,2048,2048]{2,1,0:T(8,128)(2,1)} %all-gather.5.cloned.1.call-done), kind=kLoop, calls=%fused_computation.422 | loop fusion | bytes 100663296 | tf_op jit(solution)/shard_map/slice | solution.py:131
  506.2 32.8 %copy.137 = bf16[6,2048,1024]{1,2,0:T(8,128)(2,1)} copy(bf16[6,2048,1024]{2,1,0:T(8,128)(2,1)} %get-tuple-element.63) | data formatting | bytes 50331648 | tf_op jit(solution)/shard_map/reshape | solution.py:132
  539.0 19.8 %multiply_reduce_fusion.3 = (f32[6,4,128]{2,1,0:T(4,128)S(1)}, f32[6,4,128,2048]{3,2,1,0:T(8,128)}) fusion(bf16[6,256,4,8,256]{4,3,2,1,0:T(8,128)(2,1)} %bitcast.273, bf16[6,16,4,8,256]{4,3,2,1,0:T(8,128)(2,1)} %bitcast.286), kind=kOutput, calls=%fused_computation.20 | convolution fusion | flops 3233805312 | bytes 51916800 | tf_op jit(solution)/shard_map/rqhd,rkhd->rhqk/dot_general | solution.py:134
  558.8 15.1 %exponential_reduce_fusion.1 = (f32[6,4,128]{2,1,0:T(4,128)}, f32[6,4,128]{2,1,0:T(4,128)S(1)}) fusion(f32[6,4,128,2048]{3,2,1,0:T(8,128)} %get-tuple-element.123, f32[6,4,128]{2,1,0:T(4,128)S(1)} %is-finite_select_fusion.1, f32[6,4,128]{2,1,0:T(4,128)S(1)} %get-tuple-element.122), kind=kLoop, calls=%fused_computation.12 | loop fusion | flops 31451136 | bytes 25214976 | tf_op jit(solution)/shard_map/reduce_sum | solution.py:251
  573.9 18.7 %fusion.64 = bf16[6,4,256,128]{3,2,1,0:T(8,128)(2,1)S(1)} fusion(bf16[6,2048,4,256]{1,3,2,0:T(8,128)(2,1)} %bitcast.274, f32[6,4,128,2048]{3,2,1,0:T(8,128)} %get-tuple-element.123, f32[6,4,128]{2,1,0:T(4,128)S(1)} %get-tuple-element.10, f32[6,4,128]{2,1,0:T(4,128)S(1)} %get-tuple-element.122), kind=kOutput, calls=%fused_computation.91 | convolution fusion | flops 3247177728 | bytes 51929088 | tf_op jit(solution)/shard_map/rhqk,rkhd->rqhd/dot_general | solution.py:144
  595.4 16.7 %fusion.39 = (u8[128,4096]{1,0:T(8,128)(4,1)S(1)}, u8[128,4096]{1,0:T(8,128)(4,1)S(1)}, f32[6,128,4096]{2,1,0:T(8,128)}) fusion(f32[4096]{0:T(1024)S(1)} %slice.440, bf16[1024,4096]{1,0:T(8,128)(2,1)} %param.34, f32[6,128,1024]{2,1,0:T(8,128)S(1)} %get-tuple-element.125, f32[1024]{0:T(1024)S(1)} %get-tuple-element.156, f32[1024]{0:T(1024)S(1)} %get-tuple-element.110, ...), kind=kOutput, calls=%fused_computation.69 | convolution fusion | flops 6489374720 | bytes 25196544 | tf_op jit(solution)/shard_map/dot_general | solution.py:97
  612.1 39.3 %fusion.264 = (f32[6,128]{1,0:T(8,128)S(1)}, f32[6,128,1024]{2,1,0:T(8,128)S(1)}) fusion(f32[1024]{0:T(1024)S(1)} %get-tuple-element.82, bf16[4096,1024]{1,0:T(8,128)(2,1)} %param.35, f32[6,128,4096]{2,1,0:T(8,128)} %get-tuple-element.126, f32[4096]{0:T(1024)S(1)} %slice.440, u8[128,4096]{1,0:T(8,128)(4,1)S(1)} %get-tuple-element.16, ...), kind=kOutput, calls=%fused_computation.433 | convolution fusion | flops 6671301632 | bytes 28349440 | tf_op jit(solution)/shard_map/dot_general | solution.py:97
  655.6 23.8 %multiply_reduce_fusion.1 = (f32[6,4,128]{2,1,0:T(4,128)S(1)}, f32[6,4,128]{2,1,0:T(4,128)S(1)}, f32[6,4,128,2048]{3,2,1,0:T(8,128)}) fusion(f32[6,4,128,2048]{3,2,1,0:T(8,128)} %get-tuple-element.123, f32[6,4,128]{2,1,0:T(4,128)S(1)} %get-tuple-element.10, f32[6,4,128]{2,1,0:T(4,128)S(1)} %get-tuple-element.122, bf16[6,128,4,32]{1,3,2,0:T(8,128)(2,1)S(1)} %bitcast.293, ...), kind=kOutput, calls=%fused_computation.13 | convolution fusion | flops 452978688 | bytes 53723136 | tf_op jit(solution)/shard_map/rqhd,rkhd->rhqk/dot_general | solution.py:134
  679.4 14.6 %exponential_reduce_fusion = (f32[6,4,128]{2,1,0:T(4,128)S(1)}, f32[6,4,128]{2,1,0:T(4,128)S(1)}) fusion(f32[6,4,128,2048]{3,2,1,0:T(8,128)} %get-tuple-element.131, f32[6,4,128]{2,1,0:T(4,128)S(1)} %is-finite_select_fusion, f32[6,4,128]{2,1,0:T(4,128)S(1)} %get-tuple-element.12), kind=kLoop, calls=%fused_computation.11 | loop fusion | flops 31451136 | bytes 25214976 | tf_op jit(solution)/shard_map/reduce_sum | solution.py:252
  694.0 10.8 fusion.163
  739.8 12.3 %fusion.35 = bf16[6,4,32,2048]{3,2,1,0:T(8,128)(2,1)} fusion(bf16[6,128,4,32]{1,3,2,0:T(8,128)(2,1)S(1)} %bitcast.296, f32[6,4,128,2048]{3,2,1,0:T(8,128)} %get-tuple-element.131, f32[6,4,128]{2,1,0:T(4,128)S(1)} %get-tuple-element.14, f32[6,4,128]{2,1,0:T(4,128)S(1)} %get-tuple-element.12), kind=kOutput, calls=%fused_computation.60 | convolution fusion | flops 429391872 | bytes 28532736 | tf_op jit(solution)/shard_map/rhqk,rqhd->rkhd/dot_general | solution.py:299
  762.0 34.3 %multiply_convert_fusion = bf16[6,4,32,2048]{3,2,1,0:T(8,128)(2,1)} fusion(bf16[6,128,4,32]{1,3,2,0:T(8,128)(2,1)S(1)} %bitcast.294, f32[6,128]{1,0:T(8,128)S(1)} %get-tuple-element.113, bf16[6,128,4,32]{1,3,2,0:T(8,128)(2,1)S(1)} %bitcast.297, bf16[6,2048,4,32]{1,3,2,0:T(8,128)(2,1)} %bitcast.279, f32[6,4,128,2048]{3,2,1,0:T(8,128)} %get-tuple-element.123, ...), kind=kOutput, calls=%fused_computation.51 | convolution fusion | flops 1311773696 | bytes 57068544 | tf_op jit(solution)/shard_map/rhqk,rqhd->rkhd/dot_general | solution.py:297
  801.1 33.6 %fusion.158 = bf16[6,4,32,128]{3,2,1,0:T(8,128)(2,1)S(1)} fusion(bf16[6,2048,4,32]{1,3,2,0:T(8,128)(2,1)} %bitcast.283, f32[6,128]{1,0:T(8,128)S(1)} %get-tuple-element.113, bf16[6,128,4,32]{1,3,2,0:T(8,128)(2,1)S(1)} %bitcast.298, bf16[6,2048,4,32]{1,3,2,0:T(8,128)(2,1)} %bitcast.280, f32[6,4,128,2048]{3,2,1,0:T(8,128)} %get-tuple-element.123, ...), kind=kOutput, calls=%fused_computation.249 | convolution fusion | flops 1308824576 | bytes 57068544 | tf_op jit(solution)/shard_map/rhqk,rkhd->rqhd/dot_general | solution.py:295
  841.6 67.8 %reduce-scatter.3.cloned.1.call-done = bf16[6,128,128]{2,1,0:T(8,128)(2,1)} async-done(((bf16[6,2048,128]{2,1,0:T(8,128)(2,1)}), bf16[6,128,128]{2,1,0:T(8,128)(2,1)}) %reduce-scatter.3.cloned.1.call-update) | async-done | bytes 196624 | tf_op jit(solution)/shard_map/reduce_scatter | solution.py:303
  918.7 66.5 %all-reduce.2 = f32[6016]{0:T(1024)S(1)} all-reduce(f32[6016]{0:T(1024)S(1)} %constant_dynamic-update-slice_fusion.4), channel_id=5, replica_groups=mesh['dp'=8,'fsdp'=16] {'dp','fsdp'}, use_global_device_ids=true, to_apply=%region_48.49.clone | all-reduce | flops 6016 | bytes 48128
  985.9 84.5 %all-reduce.6.cloned.1.call-done = f32[720896]{0:T(1024)} async-done(((f32[720896]{0:T(1024)}), f32[720896]{0:T(1024)}) %all-reduce.6.cloned.1.call-update) | async-done | bytes 2883600
  1073.2 64.0 %psum.37 = f32[]{:T(128)} all-reduce(f32[]{:T(128)S(6)} %add.530), channel_id=1, replica_groups=mesh['dp'=8,'fsdp'=16] {'dp','fsdp'}, use_global_device_ids=true, to_apply=%region_50.51 | all-reduce | flops 1 | bytes 8 | tf_op jit(solution)/shard_map/psum | solution.py:340
  1139.2 63.9 %all-reduce.3 = (f32[]{:T(128)}, f32[6]{0:T(128)S(1)}, f32[6]{0:T(128)S(1)}) all-reduce(f32[]{:T(128)} %get-tuple-element.114, f32[6]{0:T(128)S(1)} %get-tuple-element.39, f32[6]{0:T(128)S(1)} %get-tuple-element.38), channel_id=1, replica_groups=mesh['dp'=8,'fsdp'=16] {'dp','fsdp'}, use_global_device_ids=true, to_apply=%region_16.17 | all-reduce | flops 13 | bytes 104 | tf_op jit(solution)/shard_map/psum | solution.py:340
  (453 shorter events, 145.2 us)
Async XLA Ops:
  7.2 585.4 %copy-start = (bf16[1024,1024]{1,0:T(8,128)(2,1)S(1)}, bf16[1024,1024]{1,0:T(8,128)(2,1)}, u32[]{:S(2)}) copy-start(bf16[1024,1024]{1,0:T(8,128)(2,1)} %param.33) | copy-start | bytes 6291460
  7.2 101.2 %all-gather.9.cloned.1.call-start = ((), (), s32[]{:S(2)}) async-start(), calls=%async_computation.6 | async-start | bytes 2906112 | tf_op jit(solution)/shard_map/all_gather | solution.py:184
  8.8 211.0 %all-gather.7.cloned.1.call-start = ((), (), s32[]{:S(2)}) async-start(), calls=%async_computation.3 | async-start | bytes 6684672 | tf_op jit(solution)/shard_map/all_gather | solution.py:229
  9.7 78.0 %collective-permute-start = (s32[6,1]{1,0:T(8,128)S(1)}, s32[6,1]{1,0:T(8,128)S(1)}, u32[]{:S(2)}, u32[]{:S(2)}) collective-permute-start(s32[6,1]{1,0:T(8,128)S(1)} %get-tuple-element.118), channel_id=1, source_target_pairs={{0,1},{1,2},{2,3},{3,4},{4,5},{5,6},{6,7},{7,8},{8,9},{9,10},{10,1... | collective-permute-start | bytes 80 | tf_op jit(solution)/shard_map/ppermute | solution.py:35
  13.7 74.0 %collective-permute-start.1 = (s32[6,1]{1,0:T(8,128)S(1)}, s32[6,1]{1,0:T(8,128)S(1)}, u32[]{:S(2)}, u32[]{:S(2)}) collective-permute-start(s32[6,1]{1,0:T(8,128)S(1)} %get-tuple-element.119), channel_id=1, source_target_pairs={{1,0},{2,1},{3,2},{4,3},{5,4},{6,5},{7,6},{8,7},{9,8},{10,9},{11,1... | collective-permute-start | bytes 80 | tf_op jit(solution)/shard_map/ppermute | solution.py:36
  128.3 85.6 %copy-start.43 = (bf16[6,128,384]{2,1,0:T(8,128)(2,1)}, bf16[6,128,384]{2,1,0:T(8,128)(2,1)S(1)}, u32[]{:S(2)}) copy-start(bf16[6,128,384]{2,1,0:T(8,128)(2,1)S(1)} %fusion.146) | copy-start | bytes 1769476
  129.2 343.8 %all-gather.5.cloned.1.call-start = ((), (), s32[]{:S(2)}) async-start(), calls=%async_computation.2 | async-start | bytes 53477376 | tf_op jit(solution)/shard_map/all_gather | solution.py:228
  140.4 67.5 %copy-start.88 = (f32[2560]{0:T(1024)S(1)}, f32[2560]{0:T(1024)}, u32[]{:S(2)}) copy-start(f32[2560]{0:T(1024)} %param.39) | copy-start | bytes 30724
  140.4 67.5 %copy-start.89 = (f32[2560]{0:T(1024)S(1)}, f32[2560]{0:T(1024)}, u32[]{:S(2)}) copy-start(f32[2560]{0:T(1024)} %param.38) | copy-start | bytes 30724
  140.4 701.3 %reduce-scatter.5.cloned.1.call-start = ((), (), s32[]{:S(2)}) async-start(), calls=%async_computation.5 | async-start | bytes 3342336 | tf_op jit(solution)/shard_map/reduce_scatter | solution.py:309
  756.9 152.6 %reduce-scatter.3.cloned.1.call-start = ((), (), s32[]{:S(2)}) async-start(), calls=%async_computation.4 | async-start | bytes 3342336 | tf_op jit(solution)/shard_map/reduce_scatter | solution.py:303
  801.0 269.4 %all-reduce.6.cloned.1.call-start = ((), (), s32[]{:S(2)}) async-start(), calls=%async_computation.7 | async-start | bytes 5767168
  841.1 68.4 %copy-start.63 = (bf16[128,384,1]{1,0,2:T(8,128)(2,1)S(1)}, bf16[128,384,1]{1,0,2:T(8,128)(2,1)}, u32[]{:S(2)}) copy-start(bf16[128,384,1]{1,0,2:T(8,128)(2,1)} %reshape.428) | copy-start | bytes 294916
  841.6 69.6 %copy-start.6 = (bf16[6,128,512]{2,1,0:T(8,128)(2,1)S(1)}, bf16[6,128,512]{2,1,0:T(8,128)(2,1)}, u32[]{:S(2)}) copy-start(bf16[6,128,512]{2,1,0:T(8,128)(2,1)} %copy-done.4) | copy-start | bytes 2359300
  917.1 287.4 %copy-start.1 = (bf16[1024,1024]{1,0:T(8,128)(2,1)S(1)}, bf16[1024,1024]{1,0:T(8,128)(2,1)}, u32[]{:S(2)}) copy-start(bf16[1024,1024]{1,0:T(8,128)(2,1)} %param.33) | copy-start | bytes 6291460
  917.3 220.6 %copy-start.64 = (f32[5632]{0:T(1024)S(1)}, f32[5632]{0:T(1024)}, u32[]{:S(2)}) copy-start(f32[5632]{0:T(1024)} %param.40) | copy-start | bytes 67588
  917.3 220.6 %copy-start.78 = (f32[5632]{0:T(1024)S(1)}, f32[5632]{0:T(1024)}, u32[]{:S(2)}) copy-start(f32[5632]{0:T(1024)} %param.42) | copy-start | bytes 67588
  917.3 220.6 %copy-start.79 = (f32[5632]{0:T(1024)S(1)}, f32[5632]{0:T(1024)}, u32[]{:S(2)}) copy-start(f32[5632]{0:T(1024)} %param.43) | copy-start | bytes 67588
  917.3 221.5 %copy-start.111 = (s32[6]{0:T(128)S(1)}, s32[6]{0:T(128)}, u32[]{:S(2)}) copy-start(s32[6]{0:T(128)} %constant.36.clone) | copy-start | bytes 76
  917.4 221.5 %copy-start.112 = (s32[6]{0:T(128)S(1)}, s32[6]{0:T(128)}, u32[]{:S(2)}) copy-start(s32[6]{0:T(128)} %constant.37.clone) | copy-start | bytes 76
  917.4 285.9 %copy-start.140 = (f32[47]{0:T(128)S(1)}, f32[47]{0:T(128)}, u32[]{:S(2)}) copy-start(f32[47]{0:T(128)} %param.41) | copy-start | bytes 568
  917.4 285.9 %copy-start.141 = (f32[47]{0:T(128)S(1)}, f32[47]{0:T(128)}, u32[]{:S(2)}) copy-start(f32[47]{0:T(128)} %param.44) | copy-start | bytes 568
  917.4 285.9 %copy-start.142 = (f32[47]{0:T(128)S(1)}, f32[47]{0:T(128)}, u32[]{:S(2)}) copy-start(f32[47]{0:T(128)} %param.45) | copy-start | bytes 568
  1138.8 65.7 %copy-start.70 = (f32[5632]{0:T(1024)}, f32[5632]{0:T(1024)S(1)}, u32[]{:S(2)}) copy-start(f32[5632]{0:T(1024)S(1)} %get-tuple-element.47) | copy-start | bytes 67588
  (134 other events, 764.7 us)
Sparse Core Ops, SparseCore 0:
  11.7 69.3 all-gather.8
  129.4 59.1 all-gather.6
  190.7 282.2 all-gather.4
  757.0 73.9 reduce-scatter.4
  834.2 75.1 reduce-scatter.2
  917.6 152.8 all-reduce.5
where the time goes:
time: 1220 us; the launch traced here: 1210 us
  waiting for transfers between devices  390 us (32%)
  blocking collectives  328 us (27%)
  matrix products  258 us (21%)
  local copies, waits for them, and re-layouts  140 us (11%)
  other arithmetic  70.7 us (6%)
  between operations  19.8 us (2%)
    all_gather x1, waiting for transfers between devices, per_device(): lax.all_gather(t_own, 'fsdp', axis=1, tiled=True)  238 us
    unnamed x2, blocking collectives  136 us
    psum x2, blocking collectives, per_device(): lax.psum((loss_local, square_g, square_w), ('dp', 'fsdp'))  128 us
    dot_general x20, matrix products, matmul(): return jnp.dot(left, right, preferred_element_type=jnp.float32)  86.2 us
    unnamed x7, waiting for transfers between devices  84.6 us
    reduce_scatter x1, waiting for transfers between devices, per_device(): lax.psum_scatter(d_keys.reshape(rows, seq_len, D_S).astype(jnp.bfloat16),...  67.8 us
    psum x1, blocking collectives, per_device(): query_count = lax.psum(count_local, ('dp', 'fsdp'))  64.3 us
    slice x3, local copies, waits for them, and re-layouts, attend(): keys = pairs[..., :width].reshape(rows, pairs.shape[1], HEADS, -1)  44.1 us
  transfers between devices with their start and end apart: 8, of which 3 were waited for; matrix products, arithmetic and copies ran while one was open for 12% of the time, Pallas kernels for 0%

commit v1 on v0

v1 whole, which is shorter than its diff:
```python
import functools
import math

import jax
import jax.numpy as jnp
from jax import lax
from jax.experimental import pallas as pl
from jax.experimental.pallas import tpu as pltpu
from jax.sharding import PartitionSpec as P

D_E = 512
D_T = 1024
FF_T = 4096
D_S = 128
FF_S = 512
HEADS = 4
FFN_COUNT = 4
STEP = 5
HEAD_T = 256
HEAD_S = 32
SEQ = 2048
QB = 256
OWN = 3 * QB
SLOTS = 2 * SEQ

CLIP_NORM = 0.05
BETA_ONE = 0.9
BETA_TWO = 0.999
LEARN_RATE = 0.3
WEIGHT_DECAY = 0.01
ADAM_EPS = 1e-06

F32 = jnp.float32
BF16 = jnp.bfloat16
LOG2E = 1.4426950408889634
MESH = pl.DeviceIdType.MESH
BIG_VMEM = 60 * 2**20

MAT_ROWS = (512, 384, 128, 2048, 2048, 512)
SHARD = 44
BLOCK = 48
(V_IN, V_QKV, V_ATT, V_AGAIN, V_ASHIFT, V_UP, V_DOWN, V_FGAIN, V_FSHIFT, V_OUT, V_OGAIN, V_OSHIFT) = (
    0, 1, 4, 5, 6, 7, 23, 27, 31, 35, 39, 43)


def dot(left, right):
    return jnp.dot(left, right, preferred_element_type=F32)


def dot_nt(left, right):
    return lax.dot_general(left, right, (((1,), (1,)), ((), ())), preferred_element_type=F32)


def dot_tn(left, right):
    return lax.dot_general(left, right, (((0,), (0,)), ((), ())), preferred_element_type=F32)


def layer_norm(values, gain, shift):
    center = values - jnp.mean(values, -1, keepdims=True)
    spread = jnp.mean(center * center, -1, keepdims=True)
    return center * lax.rsqrt(spread + 1e-05) * gain + shift


def gelu(values):
    return 0.5 * values * (1.0 + lax.erf(values * 0.7071067811865476))


def params(**more):
    return pltpu.CompilerParams(vmem_limit_bytes=BIG_VMEM, **more)


def whole(*shape):
    return pl.BlockSpec(shape, lambda *_: (0,) * len(shape))


def rows_of(place):
    i, g = place % 8, place // 8
    return 3 * g + (3 * i) // 8, 3 * g + (3 * i + 2) // 8


def spread_kernel(e_ref, mask_ref, all_ref, weight_ref, masks, send, recv):
    dp, me = lax.axis_index("dp"), lax.axis_index("fsdp")
    barrier = pltpu.get_barrier_semaphore()

    def greet(k, _):
        pl.semaphore_signal(barrier, inc=1, device_id=(dp, (me + k) % 16), device_id_type=MESH)
        return 0

    lax.fori_loop(1, 16, greet, 0)
    r0, r1 = rows_of(me)
    all_ref[0, me] = e_ref[r0]
    masks[me] = mask_ref[...]

    @pl.when(r1 == r0)
    def _():
        all_ref[1] = jnp.zeros_like(all_ref[1])

    @pl.when(r1 != r0)
    def _():
        all_ref[1, me] = e_ref[r1]

    pl.semaphore_wait(barrier, 15)

    def copies(k):
        peer = (me + k) % 16
        s0, s1 = rows_of(peer)
        where = dict(device_id=(dp, peer), device_id_type=MESH)
        return (
            pltpu.make_async_remote_copy(e_ref.at[s0], all_ref.at[0, me], send.at[k, 0], recv.at[k, 0], **where),
            pltpu.make_async_remote_copy(e_ref.at[s1], all_ref.at[1, me], send.at[k, 1], recv.at[k, 1], **where),
            pltpu.make_async_remote_copy(mask_ref, masks.at[me], send.at[k, 2], recv.at[k, 2], **where),
            s0 != s1,
        )

    def start(k, _):
        first, second, third, two = copies(k)
        first.start()
        third.start()

        @pl.when(two)
        def _():
            second.start()

        return 0

    lax.fori_loop(1, 16, start, 0)

    def finish(k, _):
        first, second, third, two = copies(k)
        first.wait_send()
        third.wait_send()

        @pl.when(two)
        def _():
            second.wait_send()

        source = (me + 16 - k) % 16
        here = dict(device_id=(dp, source), device_id_type=MESH)
        pltpu.make_async_remote_copy(e_ref.at[r0], all_ref.at[0, source], send.at[k, 0], recv.at[k, 0], **here).wait_recv()
        pltpu.make_async_remote_copy(mask_ref, masks.at[source], send.at[k, 2], recv.at[k, 2], **here).wait_recv()

        @pl.when(r1 != r0)
        def _():
            pltpu.make_async_remote_copy(
                e_ref.at[r1], all_ref.at[1, source], send.at[k, 1], recv.at[k, 1], **here
            ).wait_recv()

        return 0

    lax.fori_loop(1, 16, finish, 0)
    first_block = (3 * (me % 8)) % 8
    for j in range(3):
        t = first_block + j
        row = lax.select(t >= 8, r1, r0)
        for half in range(2):
            line = masks[2 * (t % 8) + half, pl.ds(row, 1), :]
            weight_ref[j, :, half * 128 : half * 128 + 128] = line.astype(F32)


def spread(rows, mask):
    vmem = pl.BlockSpec(memory_space=pltpu.VMEM)
    return pl.pallas_call(
        spread_kernel,
        in_specs=[vmem] * 2,
        out_specs=[vmem] * 2,
        out_shape=[
            jax.ShapeDtypeStruct((2, 16, 128, 128), BF16),
            jax.ShapeDtypeStruct((3, 1, QB), F32),
        ],
        scratch_shapes=[
            pltpu.VMEM((16, 8, 128), jnp.int32),
            pltpu.SemaphoreType.DMA((16, 3)),
            pltpu.SemaphoreType.DMA((16, 3)),
        ],
        compiler_params=params(collective_id=0, has_side_effects=True),
        name="spread",
    )(rows, mask)


PT = 512


def project_kernel(meta, e_ref, proj_ref, ebias_ref, types_ref, win_ref, wkv_ref, bias_ref, emb_ref, k_ref, vt_ref):
    t = pl.program_id(0)
    per = SEQ // PT
    s, p = t // per, t % per
    base = t * PT
    mid = e_ref[pl.ds(pl.multiple_of(base, PT), PT), :]
    lo, hi = jnp.maximum(base - 16, 0), jnp.minimum(base + PT, SLOTS - 16)
    before = e_ref[pl.ds(pl.multiple_of(lo, 16), 16), :].astype(F32)[15:16]
    after = e_ref[pl.ds(pl.multiple_of(hi, 16), 16), :].astype(F32)[0:1]
    before = jnp.where(p == 0, 0.0, before)
    after = jnp.where(p == per - 1, 0.0, after)
    wide = mid.astype(F32)
    row = lax.broadcasted_iota(jnp.int32, (PT, 1), 0)
    left = jnp.where(row == 0, before, pltpu.roll(wide, 1, 0)).astype(BF16)
    right = jnp.where(row == PT - 1, after, pltpu.roll(wide, PT - 1, 0)).astype(BF16)
    trigram = jnp.concatenate([left, mid, right], 1)
    split = jnp.where(s == 0, meta[0], meta[1])
    typed = jnp.where(row + p * PT >= split, types_ref[1:2, :], types_ref[0:1, :])
    emb = (dot(trigram, proj_ref[...]) + ebias_ref[...] + typed).astype(BF16)
    emb_ref[...] = emb
    hidden = (dot(emb, win_ref[...]) + bias_ref[:, :D_T]).astype(BF16)
    k_ref[...] = (dot(hidden, wkv_ref[:, D_T : 2 * D_T]) + bias_ref[:, 2 * D_T : 3 * D_T]).astype(BF16)
    values = (dot(hidden, wkv_ref[:, 2 * D_T :]) + bias_ref[:, 3 * D_T : 4 * D_T]).astype(BF16)
    vt_ref[...] = values.T


def project(meta, e, proj, ebias, types, win, wqkv, bias):
    return pl.pallas_call(
        project_kernel,
        grid_spec=pltpu.PrefetchScalarGridSpec(
            num_scalar_prefetch=1,
            grid=(SLOTS // PT,),
            in_specs=[
                whole(SLOTS, 128),
                whole(3 * 128, D_E),
                whole(1, D_E),
                whole(2, D_E),
                whole(D_E, D_T),
                whole(D_T, 3 * D_T),
                whole(1, 10752),
            ],
            out_specs=[
                pl.BlockSpec((PT, D_E), lambda t, m: (t, 0)),
                pl.BlockSpec((PT, D_T), lambda t, m: (t, 0)),
                pl.BlockSpec((D_T, PT), lambda t, m: (0, t)),
            ],
        ),
        out_shape=[
            jax.ShapeDtypeStruct((SLOTS, D_E), BF16),
            jax.ShapeDtypeStruct((SLOTS, D_T), BF16),
            jax.ShapeDtypeStruct((D_T, SLOTS), BF16),
        ],
        compiler_params=params(),
        name="project",
    )(meta, e, proj, ebias, types, win, wqkv, bias)


def own_kernel(meta, emb_all, win_ref, wqkv_ref, bias_ref, emb_ref, hid_ref, q_ref, sem):
    copy = pltpu.make_async_copy(emb_all.at[pl.ds(pl.multiple_of(meta[2] * QB, QB), OWN)], emb_ref, sem)
    copy.start()
    copy.wait()
    hidden = dot(emb_ref[...], win_ref[...]) + bias_ref[:, :D_T]
    hid_ref[...] = hidden
    queries = (dot(hidden.astype(BF16), wqkv_ref[...]) + bias_ref[:, D_T : 2 * D_T]).astype(BF16)
    q_ref[...] = queries * jnp.asarray(HEAD_T**-0.5, BF16)


def own_queries(meta, emb, win, wqkv, bias):
    return pl.pallas_call(
        own_kernel,
        grid_spec=pltpu.PrefetchScalarGridSpec(
            num_scalar_prefetch=1,
            grid=(1,),
            in_specs=[
                pl.BlockSpec(memory_space=pl.ANY),
                whole(D_E, D_T),
                whole(D_T, D_T),
                whole(1, 10752),
            ],
            out_specs=[whole(OWN, D_E), whole(OWN, D_T), whole(OWN, D_T)],
            scratch_shapes=[pltpu.SemaphoreType.DMA],
        ),
        out_shape=[
            jax.ShapeDtypeStruct((OWN, D_E), BF16),
            jax.ShapeDtypeStruct((OWN, D_T), F32),
            jax.ShapeDtypeStruct((OWN, D_T), BF16),
        ],
        compiler_params=params(),
        name="own_queries",
    )(meta, emb, win, wqkv, bias)


ST = 1024


def student_in_kernel(emb_ref, win_ref, wqkv_ref, vec_ref, first_ref, q_ref, k_ref, v_ref, kt_ref, vt_ref):
    first = (dot(emb_ref[...], win_ref[...]) + vec_ref[V_IN : V_IN + 1, :]).astype(BF16)
    first_ref[...] = first
    qkv = dot(first, wqkv_ref[...])
    q_ref[...] = (qkv[:, :D_S] + vec_ref[V_QKV : V_QKV + 1, :]).astype(BF16)
    keys = (qkv[:, D_S : 2 * D_S] + vec_ref[V_QKV + 1 : V_QKV + 2, :]).astype(BF16)
    values = (qkv[:, 2 * D_S :] + vec_ref[V_QKV + 2 : V_QKV + 3, :]).astype(BF16)
    k_ref[...] = keys
    v_ref[...] = values
    kt_ref[...] = keys.T
    vt_ref[...] = values.T


def student_in(emb, win, wqkv, vecs):
    tall = jax.ShapeDtypeStruct((SLOTS, D_S), BF16)
    flat = jax.ShapeDtypeStruct((D_S, SLOTS), BF16)
    down = pl.BlockSpec((ST, D_S), lambda t: (t, 0))
    across = pl.BlockSpec((D_S, ST), lambda t: (0, t))
    return pl.pallas_call(
        student_in_kernel,
        grid=(SLOTS // ST,),
        in_specs=[pl.BlockSpec((ST, D_E), lambda t: (t, 0)), whole(D_E, D_S), whole(D_S, 3 * D_S), whole(48, 128)],
        out_specs=[down, down, down, down, across, across],
        out_shape=[tall, tall, tall, tall, flat, flat],
        compiler_params=params(),
        name="student_in",
    )(emb, win, wqkv, vecs)


CK = 64


def head_lanes(values, head):
    lane = lax.broadcasted_iota(jnp.int32, (1, D_S), 1)
    return jnp.where(lane // HEAD_S == head, values, jnp.zeros_like(values))


def attend_kernel(meta, tq_ref, tk_ref, tvt_ref, sq_ref, sk_ref, svt_ref, et_ref, es_ref, tmix_ref, smix_ref, stat_ref, ts, ss):
    head = pl.program_id(1)
    s_scale = HEAD_S**-0.5
    queries = tq_ref[...]
    s_queries = head_lanes(sq_ref[...], head)
    t_max = jnp.full((8, QB), -jnp.inf, F32)
    s_max = jnp.full((8, QB), -jnp.inf, F32)
    for c in range(SEQ // 256):
        part = pl.ds(c * 256, 256)
        t_part = dot_nt(tk_ref[part, :], queries)
        ts[part, :] = t_part
        t_max = jnp.maximum(t_max, jnp.max(t_part.reshape(32, 8, QB), 0))
        s_part = dot_nt(sk_ref[part, :], s_queries)
        ss[part, :] = s_part
        s_max = jnp.maximum(s_max, jnp.max(s_part.reshape(32, 8, QB), 0))
    t_top = jnp.max(t_max, 0, keepdims=True)
    s_top = jnp.max(s_max, 0, keepdims=True)
    t_off, s_off = t_top * LOG2E, s_top * (s_scale * LOG2E)

    def step(c, carry):
        t_sum, s_sum, kl = carry
        part = pl.ds(pl.multiple_of(c * CK, CK), CK)
        t_part, s_part = ts[part, :], ss[part, :]
        t_exp = jnp.exp2(t_part * LOG2E - t_off)
        s_exp = jnp.exp2(s_part * (s_scale * LOG2E) - s_off)
        et_ref[0, 0, part, :] = t_exp.astype(BF16)
        es_ref[0, 0, part, :] = s_exp.astype(BF16)
        fold = lambda v: jnp.sum(v.reshape(CK // 8, 8, QB), 0)
        return (
            t_sum + fold(t_exp),
            s_sum + fold(s_exp),
            kl + fold(t_exp * (t_part - s_part * s_scale)),
        )

    zero = jnp.zeros((8, QB), F32)
    t_sum, s_sum, kl = lax.fori_loop(0, SEQ // CK, step, (zero, zero, zero), unroll=2)
    t_sum = jnp.sum(t_sum, 0, keepdims=True)
    s_sum = jnp.sum(s_sum, 0, keepdims=True)
    kl = jnp.sum(kl, 0, keepdims=True)
    t_inv, s_inv = 1.0 / t_sum, 1.0 / s_sum
    kl = kl * t_inv - (t_top + jnp.log(t_sum)) + (s_top * s_scale + jnp.log(s_sum))
    stat_ref[0, 0, 0:1, :] = t_inv
    stat_ref[0, 0, 1:2, :] = s_inv
    stat_ref[0, 0, 2:3, :] = kl
    stat_ref[0, 0, 3:8, :] = jnp.zeros((5, QB), F32)
    t_mixed = dot(tvt_ref[...], et_ref[0, 0]) * t_inv
    tmix_ref[...] = t_mixed.T.astype(BF16)
    smix_ref[0] = dot(svt_ref[...], es_ref[0, 0]) * s_inv


def attend(meta, tq, tk, tvt, sq, sk, svt):
    slot = lambda j, m: (m[2] + j) // 8
    return pl.pallas_call(
        attend_kernel,
        grid_spec=pltpu.PrefetchScalarGridSpec(
            num_scalar_prefetch=1,
            grid=(3, HEADS),
            in_specs=[
                pl.BlockSpec((QB, HEAD_T), lambda j, h, m: (j, h)),
                pl.BlockSpec((SEQ, HEAD_T), lambda j, h, m: (slot(j, m), h)),
                pl.BlockSpec((HEAD_T, SEQ), lambda j, h, m: (h, slot(j, m))),
                pl.BlockSpec((QB, D_S), lambda j, h, m: (m[2] + j, 0)),
                pl.BlockSpec((SEQ, D_S), lambda j, h, m: (slot(j, m), 0)),
                pl.BlockSpec((HEAD_S, SEQ), lambda j, h, m: (h, slot(j, m))),
            ],
            out_specs=[
                pl.BlockSpec((1, 1, SEQ, QB), lambda j, h, m: (j, h, 0, 0)),
                pl.BlockSpec((1, 1, SEQ, QB), lambda j, h, m: (j, h, 0, 0)),
                pl.BlockSpec((QB, HEAD_T), lambda j, h, m: (j, h)),
                pl.BlockSpec((1, HEAD_S, QB), lambda j, h, m: (j, h, 0)),
                pl.BlockSpec((1, 1, 8, QB), lambda j, h, m: (j, h, 0, 0)),
            ],
            scratch_shapes=[pltpu.VMEM((SEQ, QB), F32), pltpu.VMEM((SEQ, QB), F32)],
        ),
        out_shape=[
            jax.ShapeDtypeStruct((3, HEADS, SEQ, QB), BF16),
            jax.ShapeDtypeStruct((3, HEADS, SEQ, QB), BF16),
            jax.ShapeDtypeStruct((OWN, D_T), BF16),
            jax.ShapeDtypeStruct((3, D_S, QB), F32),
            jax.ShapeDtypeStruct((3, HEADS, 8, QB), F32),
        ],
        compiler_params=params(),
        name="attend",
    )(meta, tq, tk, tvt, sq, sk, svt)


FC = 1024


def teacher_kernel(mix_ref, hid_ref, emb_ref, att_ref, up_ref, down_ref, out_ref, bias_ref, up_bias_ref, gain_ref, shift_ref, target_ref, norm, low, acc):
    c = pl.program_id(0)

    @pl.when(c == 0)
    def _():
        summed = hid_ref[...] + dot(mix_ref[...], att_ref[...]) + bias_ref[:, 4096:5120]
        one = layer_norm(summed, gain_ref[:, :D_T], shift_ref[:, :D_T])
        norm[...] = one
        low[...] = one.astype(BF16)

    act = gelu(dot(low[...], up_ref[...]) + up_bias_ref[...]).astype(BF16)
    part = dot(act, down_ref[...])

    @pl.when(c == 0)
    def _():
        acc[...] = part

    @pl.when(c > 0)
    def _():
        acc[...] += part

    @pl.when(c == pl.num_programs(0) - 1)
    def _():
        summed = norm[...] + acc[...] + bias_ref[:, 9216:10240]
        two = layer_norm(summed, gain_ref[:, D_T : 2 * D_T], shift_ref[:, D_T : 2 * D_T])
        last = emb_ref[...].astype(F32) + dot(two.astype(BF16), out_ref[...]) + bias_ref[:, 10240:]
        target_ref[...] = layer_norm(last, gain_ref[:, 2 * D_T :], shift_ref[:, 2 * D_T :])


def teacher(mix, hid, emb, att, up, down, out, bias, gain, shift):
    return pl.pallas_call(
        teacher_kernel,
        grid=(FF_T // FC,),
        in_specs=[
            whole(OWN, D_T),
            whole(OWN, D_T),
            whole(OWN, D_E),
            whole(D_T, D_T),
            pl.BlockSpec((D_T, FC), lambda c: (0, c)),
            pl.BlockSpec((FC, D_T), lambda c: (c, 0)),
            whole(D_T, D_E),
            whole(1, 10752),
            pl.BlockSpec((1, FC), lambda c: (0, 5120 // FC + c)),
            whole(1, 2560),
            whole(1, 2560),
        ],
        out_specs=whole(OWN, D_E),
        out_shape=jax.ShapeDtypeStruct((OWN, D_E), F32),
        scratch_shapes=[pltpu.VMEM((OWN, D_T), F32), pltpu.VMEM((OWN, D_T), BF16), pltpu.VMEM((OWN, D_T), F32)],
        compiler_params=params(),
        name="teacher",
    )(mix, hid, emb, att, up, down, out, bias, bias, gain, shift)


def student_kernel(emb_ref, smix_ref, target_ref, weight_ref, stat_ref, win_ref, watt_ref, wup_ref, wdown_ref, wout_ref, vec_ref,
                   grad_ref, vgrad_ref, dsum_ref, dmix_ref, part_ref, states, inners, outers):
    line = lambda r, n=1: jnp.concatenate([vec_ref[r + i : r + i + 1, :] for i in range(n)], 1) if n > 1 else vec_ref[r : r + 1, :]

    def put(r, value):
        for i in range(value.shape[1] // 128):
            vgrad_ref[r + i : r + i + 1, :] = value[:, i * 128 : i * 128 + 128]

    total = lambda v: jnp.sum(v.astype(F32), 0, keepdims=True)
    emb = emb_ref[...]
    source = emb.astype(F32)
    first = dot(emb, win_ref[...]) + line(V_IN)
    mixed = jnp.concatenate([smix_ref[j].T for j in range(3)], 0).astype(BF16)
    branch = dot(mixed, watt_ref[...]) + line(V_ATT)
    state = line(V_AGAIN) * (first + branch) + line(V_ASHIFT)
    for i in range(FFN_COUNT):
        states[i] = state
        inner = dot(state.astype(BF16), wup_ref[i]) + line(V_UP + 4 * i, 4)
        inners[i] = inner
        act = gelu(inner).astype(BF16)
        pre = state + dot(act, wdown_ref[i]) + line(V_DOWN + i)
        outers[i] = pre
        state = line(V_FGAIN + i) * pre + line(V_FSHIFT + i)
    state_low = state.astype(BF16)
    summed = source + dot(state_low, wout_ref[...]) + line(V_OUT, 4)
    diff = line(V_OGAIN, 4) * summed + line(V_OSHIFT, 4) - target_ref[...]
    weight = weight_ref[...]
    loss = jnp.sum(weight * jnp.sum(diff * diff, 1, keepdims=True)) * (1.0 / D_E)
    count = jnp.sum(weight)
    d_result = (weight * (2.0 / D_E)) * diff
    put(V_OGAIN, total(d_result * summed))
    put(V_OSHIFT, total(d_result))
    d_output = (d_result * line(V_OGAIN, 4)).astype(BF16)
    out_g = dot_tn(state_low, d_output)
    for n in range(4):
        grad_ref[pl.ds(4224 + n, 128, stride=4), :] = out_g[:, n * 128 : n * 128 + 128]
    put(V_OUT, total(d_output))
    d_state = dot_nt(d_output, wout_ref[...])
    for i in reversed(range(FFN_COUNT)):
        inner = inners[i]
        put(V_FGAIN + i, total(d_state * outers[i]))
        put(V_FSHIFT + i, total(d_state))
        d_sum = d_state * line(V_FGAIN + i)
        d_outer = d_sum.astype(BF16)
        half = 0.5 * (1.0 + lax.erf(inner * 0.7071067811865476))
        act = (inner * half).astype(BF16)
        slope = half + inner * jnp.exp(-0.5 * inner * inner) * 0.3989422804014327
        grad_ref[2176 + 512 * i : 2176 + 512 * (i + 1), :] = dot_tn(act, d_outer)
        d_inner = (dot_nt(d_outer, wdown_ref[i]) * slope).astype(BF16)
        up_g = dot_tn(states[i].astype(BF16), d_inner)
        for n in range(4):
            grad_ref[pl.ds(128 + 512 * i + n, 128, stride=4), :] = up_g[:, n * 128 : n * 128 + 128]
        put(V_UP + 4 * i, total(d_inner))
        put(V_DOWN + i, total(d_outer))
        d_state = d_sum + dot_nt(d_inner, wup_ref[i])
    put(V_AGAIN, total(d_state * (first + branch)))
    put(V_ASHIFT, total(d_state))
    d_sum = d_state * line(V_AGAIN)
    d_branch = d_sum.astype(BF16)
    grad_ref[0:128, :] = dot_tn(mixed, d_branch)
    put(V_ATT, total(d_branch))
    dsum_ref[...] = d_sum
    dmix_ref[...] = dot_nt(d_branch, watt_ref[...]).astype(BF16)
    for r in (0, 1, 2, 3, 47):
        vgrad_ref[r : r + 1, :] = jnp.zeros((1, 128), F32)
    kl = jnp.zeros((1, QB), F32)
    row = lax.broadcasted_iota(jnp.int32, (8, 128), 0)
    lane = lax.broadcasted_iota(jnp.int32, (8, 128), 1)
    part_ref[...] = jnp.where((row == 0) & (lane == 0), loss, 0.0) + jnp.where((row == 0) & (lane == 1), count, 0.0)


def student(emb, smix, target, weight, stat, win, watt, wup, wdown, wout, vecs):
    return pl.pallas_call(
        student_kernel,
        grid=(1,),
        in_specs=[
            whole(OWN, D_E),
            whole(3, D_S, QB),
            whole(OWN, D_E),
            whole(OWN, 1),
            whole(3, HEADS, 8, QB),
            whole(D_E, D_S),
            whole(D_S, D_S),
            whole(FFN_COUNT, D_S, FF_S),
            whole(FFN_COUNT, FF_S, D_S),
            whole(D_S, D_E),
            whole(48, 128),
        ],
        out_specs=[whole(4736, 128), whole(48, 128), whole(OWN, D_S), whole(OWN, D_S), whole(8, 128)],
        out_shape=[
            jax.ShapeDtypeStruct((4736, 128), F32),
            jax.ShapeDtypeStruct((48, 128), F32),
            jax.ShapeDtypeStruct((OWN, D_S), F32),
            jax.ShapeDtypeStruct((OWN, D_S), BF16),
            jax.ShapeDtypeStruct((8, 128), F32),
        ],
        scratch_shapes=[
            pltpu.VMEM((FFN_COUNT, OWN, D_S), F32),
            pltpu.VMEM((FFN_COUNT, OWN, FF_S), F32),
            pltpu.VMEM((FFN_COUNT, OWN, D_S), F32),
        ],
        compiler_params=params(),
        name="student",
    )(emb, smix, target, weight, stat, win, watt, wup, wdown, wout, vecs)


def back_kernel(meta, et_ref, es_ref, stat_ref, smix_ref, dmix_ref, weight_ref, sq_ref, sk_unused, sv_ref, skt_ref, dsum_ref,
                emb_ref, first_ref, wqkv_ref, grad_ref, vgrad_ref, kl_ref, dkv, dqt, ds, dq, dfirst):
    j, head = pl.program_id(0), pl.program_id(1)
    s_scale = HEAD_S**-0.5

    @pl.when((j == 0) & (head == 0))
    def _():
        dkv[...] = jnp.zeros_like(dkv)
        kl_ref[...] = jnp.zeros_like(kl_ref)

    t_inv, s_inv = stat_ref[0, 0, 0:1, :], stat_ref[0, 0, 1:2, :]
    weight = weight_ref[0]
    kl_ref[0:1, :] += weight * stat_ref[0, 0, 2:3, :] * (1.0 / HEADS)
    quarter = weight * (1.0 / HEADS)
    dmix_t = dmix_ref[...].astype(F32).T
    place = lax.broadcasted_iota(jnp.int32, (D_S, 1), 0) // HEAD_S
    dmix_t = jnp.where(place == head, dmix_t, 0.0)
    mix = smix_ref[0]
    row_dot = jnp.sum(dmix_t * jnp.concatenate([mix] * HEADS, 0), 0, keepdims=True)
    offset = row_dot - quarter
    t_part = quarter * t_inv
    dmix_low = dmix_t.astype(BF16)
    for c in range(SEQ // 256):
        part = pl.ds(c * 256, 256)
        d_probs = dot(sv_ref[part, :], dmix_low)
        es = es_ref[0, 0, part, :].astype(F32)
        et = et_ref[0, 0, part, :].astype(F32)
        ds[part, :] = ((d_probs - offset) * s_inv * es - et * t_part).astype(BF16)
    slot = pl.multiple_of((meta[2] + j) // 8 * SEQ, SEQ)
    s_queries = head_lanes(sq_ref[...], head)
    dmix_z = (dmix_t * s_inv).astype(BF16)
    for c in range(SEQ // 256):
        part = pl.ds(c * 256, 256)
        rows = pl.ds(slot + c * 256, 256)
        dkv[rows, :D_S] += dot(ds[part, :], s_queries)
        dkv[rows, D_S:] += dot_nt(es_ref[0, 0, part, :], dmix_z)
    dqt[pl.ds(pl.multiple_of(head * HEAD_S, HEAD_S), HEAD_S), :] = dot(skt_ref[...], ds[...]) * s_scale

    @pl.when(head == HEADS - 1)
    def _():
        dq[pl.ds(pl.multiple_of(j * QB, QB), QB), :] = dqt[...].T

    @pl.when((j == 2) & (head == HEADS - 1))
    def _():
        qkv_w = wqkv_ref[...]
        dq_low = dq[...].astype(BF16)
        own = pl.ds(pl.multiple_of(meta[2] * QB, QB), OWN)
        q_grad = dot_tn(first_ref[own, :], dq_low)
        own_part = dsum_ref[...] + dot_nt(dq_low, qkv_w[:, :D_S])
        kv_grad = jnp.zeros((D_S, 2 * D_S), F32)
        kv_bias = jnp.zeros((1, 2 * D_S), F32)
        for c in range(8):
            part = pl.ds(c * 512, 512)
            wide = dkv[part, :]
            low = jnp.concatenate([(wide[:, :D_S] * s_scale).astype(BF16), wide[:, D_S:].astype(BF16)], 1)
            kv_grad += dot_tn(first_ref[part, :], low)
            kv_bias += jnp.sum(low.astype(F32), 0, keepdims=True)
            dfirst[part, :] = dot_nt(low, qkv_w[:, D_S:])
        dfirst[own, :] += own_part
        in_grad = jnp.zeros((D_S, D_E), F32)
        in_bias = jnp.zeros((1, D_S), F32)
        for c in range(8):
            part = pl.ds(c * 512, 512)
            low = dfirst[part, :].astype(BF16)
            in_grad += dot_tn(low, emb_ref[part, :])
            in_bias += jnp.sum(low.astype(F32), 0, keepdims=True)
        grad_ref[0:512, :] = in_grad.T
        grad_ref[pl.ds(512, 128, stride=3), :] = q_grad
        grad_ref[pl.ds(513, 128, stride=3), :] = kv_grad[:, :D_S]
        grad_ref[pl.ds(514, 128, stride=3), :] = kv_grad[:, D_S:]
        vgrad_ref[...] = jnp.zeros((8, 128), F32)
        vgrad_ref[0:1, :] = in_bias
        vgrad_ref[1:2, :] = jnp.sum(dq_low.astype(F32), 0, keepdims=True)
        vgrad_ref[2:3, :] = kv_bias[:, :D_S]
        vgrad_ref[3:4, :] = kv_bias[:, D_S:]


def back(meta, et, es, stat, smix, dmix, weight, sq, sk, sv, skt, dsum, emb, first, wqkv):
    slot = lambda j, m: (m[2] + j) // 8
    return pl.pallas_call(
        back_kernel,
        grid_spec=pltpu.PrefetchScalarGridSpec(
            num_scalar_prefetch=1,
            grid=(3, HEADS),
            in_specs=[
                pl.BlockSpec((1, 1, SEQ, QB), lambda j, h, m: (j, h, 0, 0)),
                pl.BlockSpec((1, 1, SEQ, QB), lambda j, h, m: (j, h, 0, 0)),
                pl.BlockSpec((1, 1, 8, QB), lambda j, h, m: (j, h, 0, 0)),
                pl.BlockSpec((1, HEAD_S, QB), lambda j, h, m: (j, h, 0)),
                pl.BlockSpec((QB, D_S), lambda j, h, m: (j, 0)),
                pl.BlockSpec((1, 1, QB), lambda j, h, m: (j, 0, 0)),
                pl.BlockSpec((QB, D_S), lambda j, h, m: (m[2] + j, 0)),
                pl.BlockSpec((SEQ, D_S), lambda j, h, m: (slot(j, m), 0)),
                pl.BlockSpec((SEQ, D_S), lambda j, h, m: (slot(j, m), 0)),
                pl.BlockSpec((HEAD_S, SEQ), lambda j, h, m: (h, slot(j, m))),
                whole(OWN, D_S),
                whole(SLOTS, D_E),
                whole(SLOTS, D_S),
                whole(D_S, 3 * D_S),
            ],
            out_specs=[whole(896, 128), whole(8, 128), whole(8, QB)],
            scratch_shapes=[
                pltpu.VMEM((SLOTS, 2 * D_S), F32),
                pltpu.VMEM((D_S, QB), F32),
                pltpu.VMEM((SEQ, QB), BF16),
                pltpu.VMEM((OWN, D_S), F32),
                pltpu.VMEM((SLOTS, D_S), F32),
            ],
        ),
        out_shape=[
            jax.ShapeDtypeStruct((896, 128), F32),
            jax.ShapeDtypeStruct((8, 128), F32),
            jax.ShapeDtypeStruct((8, QB), F32),
        ],
        compiler_params=params(),
        name="back",
    )(meta, et, es, stat, smix, dmix, weight, sq, sk, sv, skt, dsum, emb, first, wqkv)


def update_kernel(g_ref, part_ref, master_ref, first_ref, second_ref, new_ref, newf_ref, news_ref, scal_ref,
                  half_out, half_in, mine, block_out, blocks_in, tile_out, tiles_f, tiles_d,
                  half_sems, block_send, block_recv, f_send, f_recv, d_send, d_recv):
    dp, fs = lax.axis_index("dp"), lax.axis_index("fsdp")
    x, core = dp // 2, dp % 2
    sibling = (2 * x + 1 - core, fs)
    barrier = pltpu.get_barrier_semaphore()

    def chip(k):
        return (2 * ((x + k // 16) % 4) + core, (fs + k) % 16)

    def greet(k, _):
        pl.semaphore_signal(barrier, inc=1, device_id=chip(k), device_id_type=MESH)
        return 0

    lax.fori_loop(1, 64, greet, 0)
    for k in range(4):
        other = (2 * ((x + k) % 4) + 1 - core, fs)
        pl.semaphore_signal(barrier, inc=1, device_id=other, device_id_type=MESH)

    def split(i, _):
        half_out[i] = g_ref[i // 16, 1 - core, i % 16].astype(BF16)
        return 0

    lax.fori_loop(0, 64, split, 0)
    pl.semaphore_wait(barrier, 67)
    swap = pltpu.make_async_remote_copy(
        half_out, half_in, half_sems.at[0], half_sems.at[1], device_id=sibling, device_id_type=MESH
    )
    swap.start()
    swap.wait()

    def join(i, _):
        summed = g_ref[i // 16, core, i % 16] + half_in[i].astype(F32)
        block_out[i] = summed.astype(BF16)
        return 0

    lax.fori_loop(0, 64, join, 0)
    my_chip = x * 16 + fs
    mine[...] = g_ref[x, core, fs] + half_in[my_chip].astype(F32)

    def block_copy(k):
        xk, fk = (x + k // 16) % 4, (fs + k) % 16
        return pltpu.make_async_remote_copy(
            block_out.at[xk * 16 + fk], blocks_in.at[k], block_send.at[k], block_recv.at[k],
            device_id=(2 * xk + core, fk), device_id_type=MESH,
        )

    def start(k, _):
        block_copy(k).start()
        return 0

    lax.fori_loop(1, 64, start, 0)

    def gather(k, _):
        block_copy(k).wait()
        mine[...] += blocks_in[k].astype(F32)
        return 0

    lax.fori_loop(1, 64, gather, 0)

    row = lax.broadcasted_iota(jnp.int32, (BLOCK, 128), 0)
    lane8 = lax.broadcasted_iota(jnp.int32, (8, 128), 1)
    row8 = lax.broadcasted_iota(jnp.int32, (8, 128), 0)
    place = (dp * 16 + fs) * SHARD + row
    is_matrix = row < SHARD
    bounds = [0]
    for rows in MAT_ROWS:
        bounds.append(bounds[-1] + rows)
    members = [is_matrix & (place >= bounds[i]) & (place < bounds[i + 1]) for i in range(6)]

    def everyone(tile, turn):
        tile_out[turn, 0] = tile
        tiles_f[turn, fs] = tile

        def f_copy(k):
            return pltpu.make_async_remote_copy(
                tile_out.at[turn, 0], tiles_f.at[turn, fs], f_send.at[turn, k], f_recv.at[turn, k],
                device_id=(dp, (fs + k) % 16), device_id_type=MESH,
            )

        def d_copy(k):
            return pltpu.make_async_remote_copy(
                tile_out.at[turn, 1], tiles_d.at[turn, dp], d_send.at[turn, k], d_recv.at[turn, k],
                device_id=((dp + k) % 8, fs), device_id_type=MESH,
            )

        for k in range(1, 16):
            f_copy(k).start()
        for k in range(1, 16):
            f_copy(k).wait()
        total = tiles_f[turn, 0]
        for k in range(1, 16):
            total = total + tiles_f[turn, k]
        tile_out[turn, 1] = total
        tiles_d[turn, dp] = total
        for k in range(1, 8):
            d_copy(k).start()
        for k in range(1, 8):
            d_copy(k).wait()
        total = tiles_d[turn, 0]
        for k in range(1, 8):
            total = total + tiles_d[turn, k]
        return total

    def entry(tile, i):
        return jnp.sum(jnp.where((row8 == 0) & (lane8 == i), tile, 0.0), keepdims=True)

    def tile_of(values):
        tile = jnp.zeros((8, 128), F32)
        for i, value in values:
            tile += jnp.where((row8 == 0) & (lane8 == i), value, 0.0)
        return tile

    grad = mine[...]
    master = master_ref[...]
    squares = master * master
    tile = part_ref[...] + tile_of(
        [(2, jnp.sum(grad * grad, keepdims=True))]
        + [(3 + i, jnp.sum(jnp.where(members[i], squares, 0.0), keepdims=True)) for i in range(6)]
    )
    tile = everyone(tile, 0)
    loss, count = entry(tile, 0), entry(tile, 1)
    inverse = 1.0 / count
    norm = jnp.sqrt(entry(tile, 2)) * inverse
    factor = CLIP_NORM / jnp.maximum(norm, CLIP_NORM)
    grad = grad * inverse * factor
    first = BETA_ONE * first_ref[...] + (1.0 - BETA_ONE) * grad
    second = BETA_TWO * second_ref[...] + (1.0 - BETA_TWO) * grad * grad
    newf_ref[...] = first
    news_ref[...] = second
    ratio = first / (1.0 - BETA_ONE**STEP) / (jnp.sqrt(second / (1.0 - BETA_TWO**STEP)) + ADAM_EPS)
    ratio = ratio + jnp.where(is_matrix, WEIGHT_DECAY * master, 0.0)
    squares = ratio * ratio
    steps = everyone(tile_of([(3 + i, jnp.sum(jnp.where(members[i], squares, 0.0), keepdims=True)) for i in range(6)]), 1)
    trust = jnp.ones((BLOCK, 128), F32)
    for i in range(6):
        trust = jnp.where(members[i], jnp.sqrt(entry(tile, 3 + i)) / jnp.sqrt(entry(steps, 3 + i)), trust)
    new_ref[...] = master - LEARN_RATE * (trust * ratio)
    scal_ref[...] = tile_of([(0, loss), (1, count), (2, norm)])


def update(grads, part, master, first, second):
    vmem = pl.BlockSpec(memory_space=pltpu.VMEM)
    block = jax.ShapeDtypeStruct((BLOCK, 128), F32)
    dma = pltpu.SemaphoreType.DMA
    return pl.pallas_call(
        update_kernel,
        in_specs=[vmem] * 5,
        out_specs=[vmem] * 4,
        out_shape=[block, block, block, jax.ShapeDtypeStruct((8, 128), F32)],
        scratch_shapes=[
            pltpu.VMEM((64, BLOCK, 128), BF16),
            pltpu.VMEM((64, BLOCK, 128), BF16),
            pltpu.VMEM((BLOCK, 128), F32),
            pltpu.VMEM((64, BLOCK, 128), BF16),
            pltpu.VMEM((64, BLOCK, 128), BF16),
            pltpu.VMEM((2, 2, 8, 128), F32),
            pltpu.VMEM((2, 16, 8, 128), F32),
            pltpu.VMEM((2, 8, 8, 128), F32),
            dma((2,)),
            dma((64,)),
            dma((64,)),
            dma((2, 16)),
            dma((2, 16)),
            dma((2, 8)),
            dma((2, 8)),
        ],
        compiler_params=params(collective_id=1, has_side_effects=True),
        name="update",
    )(grads, part, master, first, second)


def pack(mats, vecs):
    return jnp.concatenate(
        [mats.reshape(SHARD, 128), jnp.pad(vecs, (0, 128 - 47)).reshape(1, 128), jnp.zeros((BLOCK - SHARD - 1, 128), mats.dtype)]
    )


def per_device(
    token_ids,
    splits,
    valid_mask,
    embed_table,
    embed_proj,
    embed_bias,
    type_table,
    teach_in,
    teach_qkv,
    teach_att,
    teach_up,
    teach_down,
    teach_out,
    teach_bias,
    teach_gain,
    teach_shift,
    matrices,
    vectors,
    matrix_first,
    matrix_second,
    vector_first,
    vector_second,
):
    master = pack(matrices, vectors)
    gathered = lax.all_gather(master.astype(BF16), ("dp", "fsdp"), axis=0, tiled=False)
    place = lax.axis_index("fsdp")
    r0, r1 = rows_of(place)
    meta = jnp.stack([splits[r0], splits[r1], (3 * (place % 8)) % 8, jnp.zeros((), jnp.int32)]).astype(jnp.int32)
    spread_rows, weights = spread(embed_table[token_ids], jnp.pad(valid_mask, ((0, 2), (0, 0))))
    bias = teach_bias.reshape(1, -1)
    emb, t_keys, t_values = project(
        meta, spread_rows.reshape(SLOTS, 128), embed_proj, embed_bias.reshape(1, -1), type_table, teach_in, teach_qkv, bias
    )
    own_emb, hidden, t_queries = own_queries(meta, emb, teach_in, teach_qkv, bias)

    flat = gathered[:, :SHARD].reshape(5632, 128)
    vecs = jnp.pad(gathered[:, SHARD, :47].reshape(47, 128).astype(F32), ((0, 1), (0, 0)))
    in_w, qkv_w, att_w = flat[:512], flat[512:896].reshape(128, 384), flat[896:1024]
    up_w = flat[1024:3072].reshape(FFN_COUNT, D_S, FF_S)
    down_w = flat[3072:5120].reshape(FFN_COUNT, FF_S, D_S)
    out_w = flat[5120:].reshape(D_S, D_E)
    first, s_q, s_k, s_v, s_kt, s_vt = student_in(emb, in_w, qkv_w, vecs)
    et, es, t_mixed, s_mixed, stat = attend(meta, t_queries, t_keys, t_values, s_q, s_k, s_vt)
    target = teacher(
        t_mixed, hidden, own_emb, teach_att, teach_up, teach_down, teach_out, bias,
        teach_gain.reshape(1, -1), teach_shift.reshape(1, -1),
    )
    grads_c, vgrads_c, d_sum, d_mixed, part = student(
        own_emb, s_mixed, target, weights.reshape(OWN, 1), stat, in_w, att_w, up_w, down_w, out_w, vecs
    )
    grads_d, vgrads_d, kl = back(
        meta, et, es, stat, s_mixed, d_mixed, weights, s_q, s_k, s_v, s_kt, d_sum, emb, first, qkv_w
    )
    part = part.at[0, 0].add(jnp.sum(kl))
    grads = jnp.concatenate([grads_d, grads_c]).reshape(128, SHARD, 128)
    vgrads = jnp.concatenate([vgrads_d[:4], vgrads_c[4:47]]).reshape(128, 1, 47)
    grads = jnp.concatenate(
        [grads, jnp.pad(vgrads, ((0, 0), (0, 0), (0, 81))), jnp.zeros((128, BLOCK - SHARD - 1, 128), F32)], 1
    ).reshape(4, 2, 16, BLOCK, 128)
    new, new_first, new_second, scalars = update(
        grads, part, master, pack(matrix_first, vector_first), pack(matrix_second, vector_second)
    )
    mats = lambda v: v[:SHARD].reshape(-1)
    vecs_of = lambda v: v[SHARD, :47]
    return (
        scalars[0, 0],
        scalars[0, 1],
        scalars[0, 2],
        mats(new),
        mats(new_first),
        mats(new_second),
        vecs_of(new),
        vecs_of(new_first),
        vecs_of(new_second),
    )


def solution(mesh):
    both = P(("dp", "fsdp"))
    return jax.shard_map(
        per_device,
        mesh=mesh,
        in_specs=(P("dp", "fsdp"), P("dp"), P("dp", "fsdp")) + (P(),) * 13 + (both,) * 6,
        out_specs=(P(), P(), P(), both, both, both, both, both, both),
        check_vma=False,
    )
```

time: 1220 us -> 280 us (0.23)
  waiting for transfers between devices: 390 us -> 2.83 us
  blocking collectives: 328 us -> 0 us
  matrix products: 258 us -> 0 us
  Pallas kernels: 0 us -> 212 us
  local copies, waits for them, and re-layouts: 140 us -> 36.2 us
  other arithmetic: 70.7 us -> 11.5 us
    dot_general x50 -> x0, matrix products: 258 us -> none  [the longest x20 86.2 us: matmul(): return jnp.dot(left, right, preferred_element_type=jnp.float32)]
    all_gather x3 -> x1, waiting for transfers between devices: 238 us -> 2.81 us  [per_device(): lax.all_gather(master.astype(BF16), ('dp', 'fsdp'), axis=0, tiled=False)]
    pallas_call x0 -> x9, Pallas kernels: none -> 212 us  [the longest x1 46.7 us: update(): pl.pallas_call(update_kernel, in_specs=[vmem] * 5, out_specs=[vmem] * 4,...]
    psum x3 -> x0, blocking collectives: 192 us -> none  [the longest x2 128 us: per_device(): lax.psum((loss_local, square_g, square_w), ('dp', 'fsdp'))]
    unnamed x2 -> x0, blocking collectives: 136 us -> none
    unnamed x7 -> x1, waiting for transfers between devices: 84.6 us -> 0.02 us
    reduce_scatter x2 -> x0, waiting for transfers between devices: 67.8 us -> none  [the longest x1 67.8 us: per_device(): lax.psum_scatter(d_keys.reshape(rows, seq_len, D_S).astype(jnp.bfloat16),...]
    slice x31 -> x8, local copies, waits for them, and re-layouts: 59.9 us -> 4.75 us  [the longest x1 1.38 us: per_device(): scalars[0, 2]]
  transfers between devices with their start and end apart: 8 -> 1, of which waited for: 3 -> 1; matrix products, arithmetic and copies ran while one was open for 12% -> 6% of each run, Pallas kernels for 0% -> 21%
where the time goes in v1:
time: 280 us; the launch traced here: 278 us
  Pallas kernels  212 us (76%)
  local copies, waits for them, and re-layouts  36.2 us (13%)
  between operations  15.6 us (6%)
  other arithmetic  11.5 us (4%)
  waiting for transfers between devices  2.83 us (1%)
    pallas_call x1, Pallas kernels, update(): pl.pallas_call(update_kernel, in_specs=[vmem] * 5, out_specs=[vmem] * 4,...  46.7 us
    pallas_call x1, Pallas kernels, attend(): pl.pallas_call(attend_kernel, grid_spec=pltpu.PrefetchScalarGridSpec(num_...  35.4 us
    pallas_call x1, Pallas kernels, project(): pl.pallas_call(project_kernel, grid_spec=pltpu.PrefetchScalarGridSpec(num...  31.5 us
    pallas_call x1, Pallas kernels, back(): pl.pallas_call(back_kernel, grid_spec=pltpu.PrefetchScalarGridSpec(num_sc...  26.8 us
    pallas_call x1, Pallas kernels, teacher(): pl.pallas_call(teacher_kernel, grid=(FF_T // FC,), in_specs=[whole(OWN, D...  25.9 us
    pallas_call x1, Pallas kernels, spread(): pl.pallas_call(spread_kernel, in_specs=[vmem] * 2, out_specs=[vmem] * 2,...  19.1 us
    pallas_call x1, Pallas kernels, student(): pl.pallas_call(student_kernel, grid=(1,), in_specs=[whole(OWN, D_E), whol...  12.4 us
    pallas_call x1, Pallas kernels, own_queries(): pl.pallas_call(own_kernel, grid_spec=pltpu.PrefetchScalarGridSpec(num_sca...  7.64 us
  transfers between devices with their start and end apart: 1, of which 1 were waited for; matrix products, arithmetic and copies ran while one was open for 6% of the time, Pallas kernels for 21%

profile of v1, /device:TPU:1, one launch (start us, length us, event | category | flops | bytes accessed | tf_op | source)
XLA Modules:
  0.0 278.5 jit_solution(16232489215536405771)
XLA Ops:
  9.5 1.4 reshape.162.bias_ref.up_bias_ref
  10.9 1.3 pad.29.mask_ref
  12.9 6.5 %gather_fusion = bf16[768,128]{1,0:T(8,128)(2,1)} fusion(bf16[30522,128]{1,0:T(8,128)(2,1)} %param.27, s32[1024]{0:T(1024)S(1)} %pad_clamp_fusion), kind=kCustom, calls=%fused_computation | custom fusion | bytes 396288 | tf_op jit(solution)/shard_map/gather | solution.py:891
  19.4 19.1 %spread.1 = (bf16[2,16,128,128]{3,2,1,0:T(8,128)(2,1)}, f32[3,1,256]{2,1,0:T(1,128)}) custom-call(bf16[6,128,128]{2,1,0:T(8,128)(2,1)} %bitcast.42, s32[8,128]{1,0:T(8,128)} %pad.29.mask_ref), custom_call_target="tpu_custom_call" | custom-call | tf_op jit(solution)/shard_map/spread/pallas_call | solution.py:162
  38.5 1.3 fusion.4
  39.8 1.9 pad_add_fusion.meta
  41.7 31.5 %project.1 = (bf16[4096,512]{1,0:T(8,128)(2,1)}, bf16[4096,1024]{1,0:T(8,128)(2,1)}, bf16[1024,4096]{1,0:T(8,128)(2,1)}) custom-call(s32[4]{0:T(128)} %pad_add_fusion.meta, bf16[4096,128]{1,0:T(8,128)(2,1)} %bitcast.41, bf16[384,512]{1,0:T(8,128)(2,1)} %proj_ref.1, f32[1,512]{1,0:T(1,128)} %bitcast.48, f32[2,512]{1,0:T(2,128)} %types_ref.1, ...), custom_call_target="tpu_custom_call" | custom-call | tf_op jit(solution)/shard_map/project/pallas_call | solution.py:210
  73.3 7.6 %own_queries.1 = (bf16[768,512]{1,0:T(8,128)(2,1)}, f32[768,1024]{1,0:T(8,128)}, bf16[768,1024]{1,0:T(8,128)(2,1)}) custom-call(s32[4]{0:T(128)} %pad_add_fusion.meta, bf16[4096,512]{1,0:T(8,128)(2,1)} %get-tuple-element.53.emb_all.emb_ref, bf16[512,1024]{1,0:T(8,128)(2,1)} %win_ref.3, bf16[1024,3072]{1,0:T(8,128)(2,1)} %wqkv_ref.1, ...), custom_call_target="tpu_custom_call" | custom-call | tf_op jit(solution)/shard_map/own_queries/pallas_call | solution.py:251
  84.0 2.8 %all-gather.2.cloned.1.call-done = bf16[128,48,128]{2,1,0:T(8,128)(2,1)} async-done(((bf16[1,48,128]{2,1,0:T(8,128)(2,1)}), bf16[128,48,128]{2,1,0:T(8,128)(2,1)}) %all-gather.2.cloned.1.call-update) | async-done | bytes 1572880 | tf_op jit(solution)/shard_map/all_gather | solution.py:887
  86.8 2.3 reshape.163
  95.8 6.8 %student_in.1 = (bf16[4096,128]{1,0:T(8,128)(2,1)}, bf16[4096,128]{1,0:T(8,128)(2,1)}, bf16[4096,128]{1,0:T(8,128)(2,1)}, bf16[4096,128]{1,0:T(8,128)(2,1)}, bf1...) custom-call(bf16[4096,512]{1,0:T(8,128)(2,1)} %get-tuple-element.53.emb_all.emb_ref, ...), custom_call_target="tpu_custom_call" | custom-call | tf_op jit(solution)/shard_map/student_in/pallas_call | solution.py:296
  102.6 35.4 %attend.1 = (bf16[3,4,2048,256]{3,2,1,0:T(8,128)(2,1)}, bf16[3,4,2048,256]{3,2,1,0:T(8,128)(2,1)}, bf16[768,1024]{1,0:T(8,128)(2,1)}, f32[3,128,256]{2,1,0:T(8,128)}, f32[3,4,8,256]{3,2,1,0:T(8,128)}) custom-call(s32[4]{0:T(128)} %pad_add_fusion.meta, bf16[768,1024]{1,0:T(8,128)(2,1)} %get-tuple-element.54.tq_ref, ...), custom_call_target="tpu_custom_call" | custom-call | tf_op jit(solution)/shard_map/attend/pallas_call | solution.py:367
  138.0 25.9 %teacher.1.target_ref = f32[768,512]{1,0:T(8,128)} custom-call(bf16[768,1024]{1,0:T(8,128)(2,1)} %get-tuple-element.65.mix_ref, f32[768,1024]{1,0:T(8,128)} %get-tuple-element.66.hid_ref, bf16[768,512]{1,0:T(8,128)(2,1)} %get-tuple-element.64.emb_ref, bf16[1024,1024]{1,0:T(8,128)(2,1)} %att_ref.1, bf16[1024,4096]{1,0:T(8,128)(2,1)} %up_ref.1, ...), custom_call_target="tpu_custom_call" | custom-call | tf_op jit(solution)/shard_map/teacher/pallas_call | solution.py:434
  163.9 12.4 %student.1 = (f32[4736,128]{1,0:T(8,128)}, f32[48,128]{1,0:T(8,128)}, f32[768,128]{1,0:T(8,128)}, bf16[768,128]{1,0:T(8,128)(2,1)}, f32[8,128]{1,0:T(8,128)}) custom-call(bf16[768,512]{1,0:T(8,128)(2,1)} %get-tuple-element.64.emb_ref, f32[3,128,256]{2,1,0:T(8,128)} %get-tuple-element.63.smix_ref, f32[768,512]{1,0:T(8,128)} %teacher.1.target_ref, ...), custom_call_target="tpu_custom_call" | custom-call | tf_op jit(solution)/shard_map/student/pallas_call | solution.py:530
  176.3 26.8 %back.1 = (f32[896,128]{1,0:T(8,128)}, f32[8,128]{1,0:T(8,128)}, f32[8,256]{1,0:T(8,128)}) custom-call(s32[4]{0:T(128)} %pad_add_fusion.meta, bf16[3,4,2048,256]{3,2,1,0:T(8,128)(2,1)} %get-tuple-element.60.et_ref, bf16[3,4,2048,256]{3,2,1,0:T(8,128)(2,1)} %get-tuple-element.61.es_ref, f32[3,4,8,256]{3,2,1,0:T(8,128)} %get-tuple-element.62.stat_ref, ...), custom_call_target="tpu_custom_call" | custom-call | tf_op jit(solution)/shard_map/back/pallas_call | solution.py:643
  203.1 1.3 reduce_sum.9
  208.2 2.8 pad_maximum_fusion
  211.0 2.6 concatenate.46
  213.9 2.1 maximum_maximum_fusion.g_ref
  215.9 46.7 %update.1 = (f32[48,128]{1,0:T(8,128)}, f32[48,128]{1,0:T(8,128)}, f32[48,128]{1,0:T(8,128)}, f32[8,128]{1,0:T(8,128)}) custom-call(f32[4,2,16,48,128]{4,3,2,1,0:T(8,128)} %maximum_maximum_fusion.g_ref, f32[8,128]{1,0:T(8,128)} %scatter-add.4.part_ref, f32[48,128]{1,0:T(8,128)} %get-tuple-element.92.master_ref, f32[48,128]{1,0:T(8,128)} %get-tuple-element.91.first_ref, ...), custom_call_target="tpu_custom_call" | custom-call | tf_op jit(solution)/shard_map/update/pallas_call | solution.py:829
  262.6 1.3 slice_bitcast_fusion
  265.2 1.3 slice_bitcast_fusion.1
  267.7 1.3 slice_bitcast_fusion.2
  270.3 1.4 fusion.3
  (61 shorter events, 18.9 us)
Async XLA Ops:
  7.2 79.6 %all-gather.2.cloned.1.call-start = ((), (), s32[]{:S(2)}) async-start(), calls=%async_computation | async-start | bytes 1585152 | tf_op jit(solution)/shard_map/all_gather | solution.py:887
  73.2 7.7 %copy-start.6 = (f32[2560]{0:T(1024)S(1)}, f32[2560]{0:T(1024)}, u32[]{:S(2)}) copy-start(f32[2560]{0:T(1024)} %param.38) | copy-start | bytes 30724
  73.2 8.3 %copy-start.7 = (f32[2560]{0:T(1024)S(1)}, f32[2560]{0:T(1024)}, u32[]{:S(2)}) copy-start(f32[2560]{0:T(1024)} %param.39) | copy-start | bytes 30724
  73.2 9.0 %copy-start.5 = (f32[3,1,256]{2,1,0:T(1,128)S(1)}, f32[3,1,256]{2,1,0:T(1,128)}, u32[]{:S(2)}) copy-start(f32[3,1,256]{2,1,0:T(1,128)} %get-tuple-element.67.weight_ref) | copy-start | bytes 9220
  73.2 10.0 %copy-start.11 = (f32[47]{0:T(128)S(1)}, f32[47]{0:T(128)}, u32[]{:S(2)}) copy-start(f32[47]{0:T(128)} %param.41) | copy-start | bytes 568
  73.3 10.0 %copy-start.9 = (f32[47]{0:T(128)S(1)}, f32[47]{0:T(128)}, u32[]{:S(2)}) copy-start(f32[47]{0:T(128)} %param.45) | copy-start | bytes 568
  73.3 10.0 %copy-start.10 = (f32[47]{0:T(128)S(1)}, f32[47]{0:T(128)}, u32[]{:S(2)}) copy-start(f32[47]{0:T(128)} %param.44) | copy-start | bytes 568
  73.3 10.0 %copy-start.1 = (f32[5632]{0:T(1024)S(1)}, f32[5632]{0:T(1024)}, u32[]{:S(2)}) copy-start(f32[5632]{0:T(1024)} %param.40) | copy-start | bytes 67588
  73.3 10.0 %copy-start.2 = (f32[5632]{0:T(1024)S(1)}, f32[5632]{0:T(1024)}, u32[]{:S(2)}) copy-start(f32[5632]{0:T(1024)} %param.43) | copy-start | bytes 67588
  73.3 10.0 %copy-start.3 = (f32[5632]{0:T(1024)S(1)}, f32[5632]{0:T(1024)}, u32[]{:S(2)}) copy-start(f32[5632]{0:T(1024)} %param.42) | copy-start | bytes 67588
  176.3 31.9 %copy-start = (f32[4736,128]{1,0:T(8,128)S(1)}, f32[4736,128]{1,0:T(8,128)}, u32[]{:S(2)}) copy-start(f32[4736,128]{1,0:T(8,128)} %get-tuple-element.74) | copy-start | bytes 7274500
  211.0 2.6 copy-start.8
  211.0 2.6 copy-start.4
Sparse Core Ops, SparseCore 0:
  11.4 75.3 all-gather.1

commit v2 on v1

v2 whole, which is shorter than its diff:
```python
import functools
import math

import jax
import jax.numpy as jnp
from jax import lax
from jax.experimental import pallas as pl
from jax.experimental.pallas import tpu as pltpu
from jax.sharding import PartitionSpec as P

D_E = 512
D_T = 1024
FF_T = 4096
D_S = 128
FF_S = 512
HEADS = 4
FFN_COUNT = 4
STEP = 5
HEAD_T = 256
HEAD_S = 32
SEQ = 2048
QB = 256
OWN = 3 * QB
SLOTS = 2 * SEQ

CLIP_NORM = 0.05
BETA_ONE = 0.9
BETA_TWO = 0.999
LEARN_RATE = 0.3
WEIGHT_DECAY = 0.01
ADAM_EPS = 1e-06

F32 = jnp.float32
BF16 = jnp.bfloat16
LOG2E = 1.4426950408889634
MESH = pl.DeviceIdType.MESH
BIG_VMEM = 60 * 2**20

MAT_ROWS = (512, 384, 128, 2048, 2048, 512)
SHARD = 44
BLOCK = 48
(V_IN, V_QKV, V_ATT, V_AGAIN, V_ASHIFT, V_UP, V_DOWN, V_FGAIN, V_FSHIFT, V_OUT, V_OGAIN, V_OSHIFT) = (
    0, 1, 4, 5, 6, 7, 23, 27, 31, 35, 39, 43)


def dot(left, right):
    return jnp.dot(left, right, preferred_element_type=F32)


def dot_nt(left, right):
    return lax.dot_general(left, right, (((1,), (1,)), ((), ())), preferred_element_type=F32)


def dot_tn(left, right):
    return lax.dot_general(left, right, (((0,), (0,)), ((), ())), preferred_element_type=F32)


def layer_norm(values, gain, shift):
    center = values - jnp.mean(values, -1, keepdims=True)
    spread = jnp.mean(center * center, -1, keepdims=True)
    return center * lax.rsqrt(spread + 1e-05) * gain + shift


def gelu(values):
    return 0.5 * values * (1.0 + lax.erf(values * 0.7071067811865476))


def params(**more):
    return pltpu.CompilerParams(vmem_limit_bytes=BIG_VMEM, **more)


def whole(*shape):
    return pl.BlockSpec(shape, lambda *_: (0,) * len(shape))


def line(ref, row, count=1):
    if count == 1:
        return ref[row : row + 1, :]
    return jnp.concatenate([ref[row + i : row + i + 1, :] for i in range(count)], 1)


def fold(values, op=jnp.sum):
    return op(values.reshape(values.shape[0] // 8, 8, values.shape[1]), 0)


def rows_of(place):
    i, g = place % 8, place // 8
    return 3 * g + (3 * i) // 8, 3 * g + (3 * i + 2) // 8


def first_block():
    return (3 * (lax.axis_index("fsdp") % 8)) % 8


def slot_of(j):
    return (first_block() + j) // 8


def spread_kernel(e_ref, mask_in, mats_ref, vecs_ref, all_ref, weight_ref, params_ref, mask_ref, masks, wide, block, send, recv, p_send, p_recv, s_send, s_recv):
    dp, me = lax.axis_index("dp"), lax.axis_index("fsdp")
    x, core = dp // 2, dp % 2
    sibling = (2 * x + 1 - core, me)
    barrier = pltpu.get_barrier_semaphore()

    def chip(k):
        return (2 * ((x + k // 16) % 4) + core, (me + k) % 16)

    def greet(k, _):
        pl.semaphore_signal(barrier, inc=1, device_id=chip(k), device_id_type=MESH)
        return 0

    lax.fori_loop(1, 64, greet, 0)
    pl.semaphore_signal(barrier, inc=1, device_id=sibling, device_id_type=MESH)
    r0, r1 = rows_of(me)
    all_ref[0, me] = e_ref[r0]
    mask_ref[0:6] = mask_in[...]
    mask_ref[6:8] = jnp.zeros((2, 128), jnp.int32)
    masks[me] = mask_ref[...]
    wide[...] = jnp.zeros((BLOCK, 128), F32)
    wide[0:SHARD, :] = mats_ref[...]
    wide[SHARD : SHARD + 1, 0:47] = vecs_ref[...]
    block[...] = wide[...].astype(BF16)
    params_ref[dp * 16 + me] = block[...]

    @pl.when(r1 == r0)
    def _():
        all_ref[1] = jnp.zeros_like(all_ref[1])

    @pl.when(r1 != r0)
    def _():
        all_ref[1, me] = e_ref[r1]

    pl.semaphore_wait(barrier, 64)

    def copies(k):
        peer = (me + k) % 16
        s0, s1 = rows_of(peer)
        where = dict(device_id=(dp, peer), device_id_type=MESH)
        return (
            pltpu.make_async_remote_copy(e_ref.at[s0], all_ref.at[0, me], send.at[k, 0], recv.at[k, 0], **where),
            pltpu.make_async_remote_copy(e_ref.at[s1], all_ref.at[1, me], send.at[k, 1], recv.at[k, 1], **where),
            pltpu.make_async_remote_copy(mask_ref, masks.at[me], send.at[k, 2], recv.at[k, 2], **where),
            s0 != s1,
        )

    def start(k, _):
        first, second, third, two = copies(k)
        first.start()
        third.start()

        @pl.when(two)
        def _():
            second.start()

        return 0

    lax.fori_loop(1, 16, start, 0)

    def param_copy(k):
        return pltpu.make_async_remote_copy(
            block, params_ref.at[dp * 16 + me], p_send.at[k], p_recv.at[k], device_id=chip(k), device_id_type=MESH
        )

    def param_start(k, _):
        param_copy(k).start()
        return 0

    lax.fori_loop(1, 64, param_start, 0)

    def to_sibling(k):
        source = 2 * ((x + 4 - k // 16) % 4) + core
        place = source * 16 + (me + 64 - k) % 16
        return pltpu.make_async_remote_copy(
            params_ref.at[place], params_ref.at[place], s_send.at[k], s_recv.at[k], device_id=sibling, device_id_type=MESH
        )

    to_sibling(0).start()

    def finish(k, _):
        first, second, third, two = copies(k)
        first.wait_send()
        third.wait_send()

        @pl.when(two)
        def _():
            second.wait_send()

        source = (me + 16 - k) % 16
        here = dict(device_id=(dp, source), device_id_type=MESH)
        pltpu.make_async_remote_copy(e_ref.at[r0], all_ref.at[0, source], send.at[k, 0], recv.at[k, 0], **here).wait_recv()
        pltpu.make_async_remote_copy(mask_ref, masks.at[source], send.at[k, 2], recv.at[k, 2], **here).wait_recv()

        @pl.when(r1 != r0)
        def _():
            pltpu.make_async_remote_copy(
                e_ref.at[r1], all_ref.at[1, source], send.at[k, 1], recv.at[k, 1], **here
            ).wait_recv()

        return 0

    lax.fori_loop(1, 16, finish, 0)

    def forward(k, _):
        param_copy(k).wait()
        to_sibling(k).start()
        return 0

    lax.fori_loop(1, 64, forward, 0)

    def forwarded(k, _):
        to_sibling(k).wait()
        return 0

    lax.fori_loop(0, 64, forwarded, 0)
    for j in range(3):
        t = first_block() + j
        row = lax.select(t >= 8, r1, r0)
        for half in range(2):
            line = masks[2 * (t % 8) + half, pl.ds(row, 1), :]
            weight_ref[j, :, half * 128 : half * 128 + 128] = line.astype(F32)


def spread(rows, mask, mats, vecs):
    vmem = pl.BlockSpec(memory_space=pltpu.VMEM)
    dma = pltpu.SemaphoreType.DMA
    return pl.pallas_call(
        spread_kernel,
        in_specs=[vmem] * 4,
        out_specs=[vmem] * 3,
        out_shape=[
            jax.ShapeDtypeStruct((2, 16, 128, 128), BF16),
            jax.ShapeDtypeStruct((3, 1, QB), F32),
            jax.ShapeDtypeStruct((128, BLOCK, 128), BF16),
        ],
        scratch_shapes=[
            pltpu.VMEM((8, 128), jnp.int32),
            pltpu.VMEM((16, 8, 128), jnp.int32),
            pltpu.VMEM((BLOCK, 128), F32),
            pltpu.VMEM((BLOCK, 128), BF16),
            dma((16, 3)),
            dma((16, 3)),
            dma((64,)),
            dma((64,)),
            dma((64,)),
            dma((64,)),
        ],
        compiler_params=params(collective_id=0, has_side_effects=True),
        name="spread",
    )(rows, mask, mats, vecs)


PT = 512
TILES = SLOTS // PT


def unpack(packed_ref, flat, win_ref, wqkv_ref, watt_ref, wup_ref, wdown_ref, wout_ref, vec_ref):
    lane = lax.broadcasted_iota(jnp.int32, (1, 128), 1)
    vec_ref[...] = jnp.zeros((48, 128), F32)
    for pair in range(64):
        both = [packed_ref[2 * pair + i].astype(F32) for i in range(2)]
        flat[88 * pair : 88 * pair + 88, :] = jnp.concatenate([b[:SHARD] for b in both], 0)
        for i in range(2):
            row, shift = divmod(47 * (2 * pair + i), 128)
            entries = both[i][SHARD : SHARD + 1, :]
            moved = pltpu.roll(entries, shift, 1) if shift else entries
            vec_ref[row : row + 1, :] += jnp.where(lane >= shift, moved, 0.0)
            if shift + 47 > 128:
                vec_ref[row + 1 : row + 2, :] += jnp.where(lane < shift, moved, 0.0)
    win_ref[...] = flat[0:512, :].astype(BF16)
    for n in range(3):
        wqkv_ref[:, n * 128 : n * 128 + 128] = flat[pl.ds(512 + n, 128, stride=3), :].astype(BF16)
    watt_ref[...] = flat[896:1024, :].astype(BF16)
    for i in range(FFN_COUNT):
        for n in range(4):
            wup_ref[i, :, n * 128 : n * 128 + 128] = flat[pl.ds(1024 + 512 * i + n, 128, stride=4), :].astype(BF16)
        wdown_ref[i] = flat[3072 + 512 * i : 3584 + 512 * i, :].astype(BF16)
    for n in range(4):
        wout_ref[:, n * 128 : n * 128 + 128] = flat[pl.ds(5120 + n, 128, stride=4), :].astype(BF16)


def project_kernel(splits_ref, e_ref, packed_ref, proj_ref, ebias_ref, types_ref, twin_ref, twqkv_ref, bias_ref,
                   emb_ref, k_ref, vt_ref, first_ref, sq_ref, sk_ref, sv_ref, skt_ref, svt_ref,
                   own_ref, hid_ref, tq_ref, win_ref, wqkv_ref, watt_ref, wup_ref, wdown_ref, wout_ref, vec_ref, flat):
    t = pl.program_id(0)

    @pl.when(t == 0)
    def _():
        unpack(packed_ref, flat, win_ref, wqkv_ref, watt_ref, wup_ref, wdown_ref, wout_ref, vec_ref)

    @pl.when(t < TILES)
    def _():
        per = SEQ // PT
        s, p = t // per, t % per
        base = t * PT
        mid = e_ref[pl.ds(pl.multiple_of(base, PT), PT), :]
        lo, hi = jnp.maximum(base - 16, 0), jnp.minimum(base + PT, SLOTS - 16)
        before = e_ref[pl.ds(pl.multiple_of(lo, 16), 16), :].astype(F32)[15:16]
        after = e_ref[pl.ds(pl.multiple_of(hi, 16), 16), :].astype(F32)[0:1]
        before = jnp.where(p == 0, 0.0, before)
        after = jnp.where(p == per - 1, 0.0, after)
        wide = mid.astype(F32)
        row = lax.broadcasted_iota(jnp.int32, (PT, 1), 0)
        left = jnp.where(row == 0, before, pltpu.roll(wide, 1, 0)).astype(BF16)
        right = jnp.where(row == PT - 1, after, pltpu.roll(wide, PT - 1, 0)).astype(BF16)
        trigram = jnp.concatenate([left, mid, right], 1)
        r0, r1 = rows_of(lax.axis_index("fsdp"))
        split = splits_ref[jnp.where(s == 0, r0, r1)]
        typed = jnp.where(row + p * PT >= split, types_ref[1:2, :], types_ref[0:1, :])
        emb = (dot(trigram, proj_ref[...]) + line(ebias_ref, 0, 4) + typed).astype(BF16)
        emb_ref[pl.ds(pl.multiple_of(base, PT), PT), :] = emb
        hidden = (dot(emb, twin_ref[...]) + line(bias_ref, 0, 8)).astype(BF16)
        k_ref[...] = (dot(hidden, twqkv_ref[:, D_T : 2 * D_T]) + line(bias_ref, 16, 8)).astype(BF16)
        values = (dot(hidden, twqkv_ref[:, 2 * D_T :]) + line(bias_ref, 24, 8)).astype(BF16)
        vt_ref[...] = values.T
        first = (dot(emb, win_ref[...]) + line(vec_ref, V_IN)).astype(BF16)
        first_ref[...] = first
        qkv = dot(first, wqkv_ref[...])
        sq_ref[...] = (qkv[:, :D_S] + line(vec_ref, V_QKV)).astype(BF16)
        s_keys = (qkv[:, D_S : 2 * D_S] + line(vec_ref, V_QKV + 1)).astype(BF16)
        s_values = (qkv[:, 2 * D_S :] + line(vec_ref, V_QKV + 2)).astype(BF16)
        sk_ref[...] = s_keys
        sv_ref[...] = s_values
        skt_ref[...] = s_keys.T
        svt_ref[...] = s_values.T

    @pl.when(t == TILES)
    def _():
        emb = emb_ref[pl.ds(pl.multiple_of(first_block() * QB, QB), OWN), :]
        own_ref[...] = emb
        hidden = dot(emb, twin_ref[...]) + line(bias_ref, 0, 8)
        hid_ref[...] = hidden
        queries = (dot(hidden.astype(BF16), twqkv_ref[:, :D_T]) + line(bias_ref, 8, 8)).astype(BF16)
        tq_ref[...] = queries * jnp.asarray(HEAD_T**-0.5, BF16)


def project(splits, e, packed, proj, ebias, types, win, wqkv, bias):
    tall = jax.ShapeDtypeStruct((SLOTS, D_S), BF16)
    flat = jax.ShapeDtypeStruct((D_S, SLOTS), BF16)
    tile = lambda t: jnp.minimum(t, TILES - 1)
    down = pl.BlockSpec((PT, D_S), lambda t: (tile(t), 0))
    across = pl.BlockSpec((D_S, PT), lambda t: (0, tile(t)))
    made = [
        ((OWN, D_E), BF16),
        ((OWN, D_T), F32),
        ((OWN, D_T), BF16),
        ((D_E, D_S), BF16),
        ((D_S, 3 * D_S), BF16),
        ((D_S, D_S), BF16),
        ((FFN_COUNT, D_S, FF_S), BF16),
        ((FFN_COUNT, FF_S, D_S), BF16),
        ((D_S, D_E), BF16),
        ((48, 128), F32),
    ]
    return pl.pallas_call(
        project_kernel,
        grid=(TILES + 1,),
        in_specs=[
            pl.BlockSpec(memory_space=pltpu.SMEM),
            whole(SLOTS, 128),
            whole(128, BLOCK, 128),
            whole(3 * 128, D_E),
            whole(4, 128),
            whole(2, D_E),
            whole(D_E, D_T),
            whole(D_T, 3 * D_T),
            whole(84, 128),
        ],
        out_specs=[
            whole(SLOTS, D_E),
            pl.BlockSpec((PT, D_T), lambda t: (tile(t), 0)),
            pl.BlockSpec((D_T, PT), lambda t: (0, tile(t))),
        ]
        + [down] * 4
        + [across] * 2
        + [whole(*shape) for shape, _ in made],
        out_shape=[
            jax.ShapeDtypeStruct((SLOTS, D_E), BF16),
            jax.ShapeDtypeStruct((SLOTS, D_T), BF16),
            jax.ShapeDtypeStruct((D_T, SLOTS), BF16),
        ]
        + [tall] * 4
        + [flat] * 2
        + [jax.ShapeDtypeStruct(*entry) for entry in made],
        scratch_shapes=[pltpu.VMEM((5632, 128), F32)],
        compiler_params=params(),
        name="project",
    )(splits, e, packed, proj, ebias, types, win, wqkv, bias)


CB = 256
SUB = 64
STEPS = 3 * HEADS


def head_lanes(values, head):
    lane = lax.broadcasted_iota(jnp.int32, (1, D_S), 1)
    return jnp.where(lane // HEAD_S == head, values, jnp.zeros_like(values))


def attend_kernel(tq_ref, tk_ref, tvt_ref, sq_ref, sk_ref, svt_ref, et_ref, es_ref, tmix_ref, smix_ref, stat_ref,
                  ts0, ts1, ss0, ss1, mx0, mx1):
    n = pl.program_id(0)
    s_factor = HEAD_S**-0.5 * LOG2E

    def work(ts, ss, mx, tr, sr, mr, scores, mixes):
        if scores:
            queries, s_queries = tq_ref[...], head_lanes(sq_ref[...], n % HEADS)
            t_max = s_max = jnp.full((8, QB), -jnp.inf, F32)
        if mixes:
            t_top, s_top = jnp.max(mr[0], 0, keepdims=True), jnp.max(mr[1], 0, keepdims=True)
            t_off, s_off = t_top * LOG2E, s_top * s_factor
            t_sum = s_sum = kl = jnp.zeros((8, QB), F32)
            t_mix, s_mix = jnp.zeros((HEAD_T, QB), F32), jnp.zeros((HEAD_S, QB), F32)
        for c in range(SEQ // CB):
            part = slice(c * CB, c * CB + CB)
            if scores:
                t_part = dot_nt(tk_ref[part, :], queries)
                ts[part, :] = t_part
                s_part = dot_nt(sk_ref[part, :], s_queries)
                ss[part, :] = s_part
                t_max = jnp.maximum(t_max, fold(t_part, jnp.max))
                s_max = jnp.maximum(s_max, fold(s_part, jnp.max))
            if mixes:
                for u in range(c * CB, c * CB + CB, SUB):
                    some = slice(u, u + SUB)
                    t_log = tr[some, :] * LOG2E - t_off
                    s_log = sr[some, :] * s_factor - s_off
                    t_exp, s_exp = jnp.exp2(t_log), jnp.exp2(s_log)
                    et_ref[0, some, :] = t_exp.astype(BF16)
                    es_ref[0, some, :] = s_exp.astype(BF16)
                    t_sum, s_sum = t_sum + fold(t_exp), s_sum + fold(s_exp)
                    kl = kl + fold(t_exp * (t_log - s_log))
                t_mix += dot(tvt_ref[:, part], et_ref[0, part, :])
                s_mix += dot(svt_ref[:, part], es_ref[0, part, :])
        if scores:
            mx[0], mx[1] = t_max, s_max
        if mixes:
            t_sum, s_sum, kl = (jnp.sum(v, 0, keepdims=True) for v in (t_sum, s_sum, kl))
            t_inv, s_inv = 1.0 / t_sum, 1.0 / s_sum
            stat_ref[0, 0, 0:1, :] = t_inv
            stat_ref[0, 0, 1:2, :] = s_inv
            stat_ref[0, 0, 2:3, :] = kl * t_inv * (1.0 / LOG2E) - jnp.log(t_sum) + jnp.log(s_sum)
            stat_ref[0, 0, 3:8, :] = jnp.zeros((5, QB), F32)
            tmix_ref[...] = (t_mix * t_inv).T.astype(BF16)
            smix_ref[0] = s_mix * s_inv

    even, odd = (ts0, ss0, mx0), (ts1, ss1, mx1)
    pl.when(n == 0)(lambda: work(*even, *odd, True, False))
    pl.when((n > 0) & (n < STEPS) & (n % 2 == 0))(lambda: work(*even, *odd, True, True))
    pl.when((n > 0) & (n < STEPS) & (n % 2 == 1))(lambda: work(*odd, *even, True, True))
    pl.when(n == STEPS)(lambda: work(*even, *odd, False, True))


def attend(tq, tk, tvt, sq, sk, svt):
    now = lambda n: jnp.minimum(n, STEPS - 1)
    last = lambda n: jnp.maximum(n - 1, 0)
    block = lambda n: n // HEADS
    head = lambda n: n % HEADS
    return pl.pallas_call(
        attend_kernel,
        grid=(STEPS + 1,),
        in_specs=[
            pl.BlockSpec((QB, HEAD_T), lambda n: (block(now(n)), head(now(n)))),
            pl.BlockSpec((SEQ, HEAD_T), lambda n: (slot_of(block(now(n))), head(now(n)))),
            pl.BlockSpec((HEAD_T, SEQ), lambda n: (head(last(n)), slot_of(block(last(n))))),
            pl.BlockSpec((QB, D_S), lambda n: (first_block() + block(now(n)), 0)),
            pl.BlockSpec((SEQ, D_S), lambda n: (slot_of(block(now(n))), 0)),
            pl.BlockSpec((HEAD_S, SEQ), lambda n: (head(last(n)), slot_of(block(last(n))))),
        ],
        out_specs=[
            pl.BlockSpec((1, SEQ, QB), lambda n: (block(last(n)), 0, head(last(n)))),
            pl.BlockSpec((1, SEQ, QB), lambda n: (block(last(n)), 0, head(last(n)))),
            pl.BlockSpec((QB, HEAD_T), lambda n: (block(last(n)), head(last(n)))),
            pl.BlockSpec((1, HEAD_S, QB), lambda n: (block(last(n)), head(last(n)), 0)),
            pl.BlockSpec((1, 1, 8, QB), lambda n: (block(last(n)), head(last(n)), 0, 0)),
        ],
        out_shape=[
            jax.ShapeDtypeStruct((3, SEQ, HEADS * QB), BF16),
            jax.ShapeDtypeStruct((3, SEQ, HEADS * QB), BF16),
            jax.ShapeDtypeStruct((OWN, D_T), BF16),
            jax.ShapeDtypeStruct((3, D_S, QB), F32),
            jax.ShapeDtypeStruct((3, HEADS, 8, QB), F32),
        ],
        scratch_shapes=[pltpu.VMEM((SEQ, QB), F32)] * 4 + [pltpu.VMEM((2, 8, QB), F32)] * 2,
        compiler_params=params(),
        name="attend",
    )(tq, tk, tvt, sq, sk, svt)


FC = 1024


def teacher_kernel(mix_ref, hid_ref, emb_ref, att_ref, up_ref, down_ref, out_ref, bias_ref, gain_ref, shift_ref, target_ref, norm, low, acc):
    c = pl.program_id(0)

    @pl.when(c == 0)
    def _():
        summed = hid_ref[...] + dot(mix_ref[...], att_ref[...]) + line(bias_ref, 32, 8)
        one = layer_norm(summed, line(gain_ref, 0, 8), line(shift_ref, 0, 8))
        norm[...] = one
        low[...] = one.astype(BF16)

    rows = FC // 128
    up_bias = bias_ref[pl.ds(pl.multiple_of(40 + rows * c, 8), rows), :]
    act = gelu(dot(low[...], up_ref[...]) + line(up_bias, 0, rows)).astype(BF16)
    part = dot(act, down_ref[...])

    @pl.when(c == 0)
    def _():
        acc[...] = part

    @pl.when(c > 0)
    def _():
        acc[...] += part

    @pl.when(c == pl.num_programs(0) - 1)
    def _():
        summed = norm[...] + acc[...] + line(bias_ref, 72, 8)
        two = layer_norm(summed, line(gain_ref, 8, 8), line(shift_ref, 8, 8))
        last = emb_ref[...].astype(F32) + dot(two.astype(BF16), out_ref[...]) + line(bias_ref, 80, 4)
        target_ref[...] = layer_norm(last, line(gain_ref, 16, 4), line(shift_ref, 16, 4))


def teacher(mix, hid, emb, att, up, down, out, bias, gain, shift):
    return pl.pallas_call(
        teacher_kernel,
        grid=(FF_T // FC,),
        in_specs=[
            whole(OWN, D_T),
            whole(OWN, D_T),
            whole(OWN, D_E),
            whole(D_T, D_T),
            pl.BlockSpec((D_T, FC), lambda c: (0, c)),
            pl.BlockSpec((FC, D_T), lambda c: (c, 0)),
            whole(D_T, D_E),
            whole(84, 128),
            whole(20, 128),
            whole(20, 128),
        ],
        out_specs=whole(OWN, D_E),
        out_shape=jax.ShapeDtypeStruct((OWN, D_E), F32),
        scratch_shapes=[pltpu.VMEM((OWN, D_T), F32), pltpu.VMEM((OWN, D_T), BF16), pltpu.VMEM((OWN, D_T), F32)],
        compiler_params=params(),
        name="teacher",
    )(mix, hid, emb, att, up, down, out, bias, gain, shift)


def student_kernel(emb_ref, smix_ref, target_ref, weight_ref, win_ref, watt_ref, wup_ref, wdown_ref, wout_ref, vec_ref,
                   grad_ref, vgrad_ref, dsum_ref, dmix_ref, part_ref, states, inners, outers):

    def put(r, value):
        for i in range(value.shape[1] // 128):
            vgrad_ref[r + i : r + i + 1, :] = value[:, i * 128 : i * 128 + 128]

    total = lambda v: jnp.sum(v.astype(F32), 0, keepdims=True)
    emb = emb_ref[...]
    source = emb.astype(F32)
    first = dot(emb, win_ref[...]) + line(vec_ref, V_IN)
    mixed = jnp.concatenate([smix_ref[j].T for j in range(3)], 0).astype(BF16)
    branch = dot(mixed, watt_ref[...]) + line(vec_ref, V_ATT)
    state = line(vec_ref, V_AGAIN) * (first + branch) + line(vec_ref, V_ASHIFT)
    for i in range(FFN_COUNT):
        states[i] = state
        inner = dot(state.astype(BF16), wup_ref[i]) + line(vec_ref, V_UP + 4 * i, 4)
        inners[i] = inner
        act = gelu(inner).astype(BF16)
        pre = state + dot(act, wdown_ref[i]) + line(vec_ref, V_DOWN + i)
        outers[i] = pre
        state = line(vec_ref, V_FGAIN + i) * pre + line(vec_ref, V_FSHIFT + i)
    state_low = state.astype(BF16)
    summed = source + dot(state_low, wout_ref[...]) + line(vec_ref, V_OUT, 4)
    diff = line(vec_ref, V_OGAIN, 4) * summed + line(vec_ref, V_OSHIFT, 4) - target_ref[...]
    weight = jnp.concatenate([jnp.broadcast_to(weight_ref[j], (8, QB)).T[:, 0:1] for j in range(3)], 0)
    loss = jnp.sum(weight * jnp.sum(diff * diff, 1, keepdims=True)) * (1.0 / D_E)
    count = jnp.sum(weight)
    d_result = (weight * (2.0 / D_E)) * diff
    put(V_OGAIN, total(d_result * summed))
    put(V_OSHIFT, total(d_result))
    d_output = (d_result * line(vec_ref, V_OGAIN, 4)).astype(BF16)
    out_g = dot_tn(state_low, d_output)
    for n in range(4):
        grad_ref[pl.ds(4224 + n, 128, stride=4), :] = out_g[:, n * 128 : n * 128 + 128]
    put(V_OUT, total(d_output))
    d_state = dot_nt(d_output, wout_ref[...])
    for i in reversed(range(FFN_COUNT)):
        inner = inners[i]
        put(V_FGAIN + i, total(d_state * outers[i]))
        put(V_FSHIFT + i, total(d_state))
        d_sum = d_state * line(vec_ref, V_FGAIN + i)
        d_outer = d_sum.astype(BF16)
        half = 0.5 * (1.0 + lax.erf(inner * 0.7071067811865476))
        act = (inner * half).astype(BF16)
        slope = half + inner * jnp.exp(-0.5 * inner * inner) * 0.3989422804014327
        grad_ref[2176 + 512 * i : 2176 + 512 * (i + 1), :] = dot_tn(act, d_outer)
        d_inner = (dot_nt(d_outer, wdown_ref[i]) * slope).astype(BF16)
        up_g = dot_tn(states[i].astype(BF16), d_inner)
        for n in range(4):
            grad_ref[pl.ds(128 + 512 * i + n, 128, stride=4), :] = up_g[:, n * 128 : n * 128 + 128]
        put(V_UP + 4 * i, total(d_inner))
        put(V_DOWN + i, total(d_outer))
        d_state = d_sum + dot_nt(d_inner, wup_ref[i])
    put(V_AGAIN, total(d_state * (first + branch)))
    put(V_ASHIFT, total(d_state))
    d_sum = d_state * line(vec_ref, V_AGAIN)
    d_branch = d_sum.astype(BF16)
    grad_ref[0:128, :] = dot_tn(mixed, d_branch)
    put(V_ATT, total(d_branch))
    dsum_ref[...] = d_sum
    dmix_ref[...] = dot_nt(d_branch, watt_ref[...]).astype(BF16)
    for r in (0, 1, 2, 3, 47):
        vgrad_ref[r : r + 1, :] = jnp.zeros((1, 128), F32)
    row = lax.broadcasted_iota(jnp.int32, (8, 128), 0)
    lane = lax.broadcasted_iota(jnp.int32, (8, 128), 1)
    part_ref[...] = jnp.where((row == 0) & (lane == 0), loss, 0.0) + jnp.where((row == 0) & (lane == 1), count, 0.0)


def student(emb, smix, target, weight, win, watt, wup, wdown, wout, vecs):
    return pl.pallas_call(
        student_kernel,
        grid=(1,),
        in_specs=[
            whole(OWN, D_E),
            whole(3, D_S, QB),
            whole(OWN, D_E),
            whole(3, 1, QB),
            whole(D_E, D_S),
            whole(D_S, D_S),
            whole(FFN_COUNT, D_S, FF_S),
            whole(FFN_COUNT, FF_S, D_S),
            whole(D_S, D_E),
            whole(48, 128),
        ],
        out_specs=[whole(4736, 128), whole(48, 128), whole(OWN, D_S), whole(OWN, D_S), whole(8, 128)],
        out_shape=[
            jax.ShapeDtypeStruct((4736, 128), F32),
            jax.ShapeDtypeStruct((48, 128), F32),
            jax.ShapeDtypeStruct((OWN, D_S), F32),
            jax.ShapeDtypeStruct((OWN, D_S), BF16),
            jax.ShapeDtypeStruct((8, 128), F32),
        ],
        scratch_shapes=[
            pltpu.VMEM((FFN_COUNT, OWN, D_S), F32),
            pltpu.VMEM((FFN_COUNT, OWN, FF_S), F32),
            pltpu.VMEM((FFN_COUNT, OWN, D_S), F32),
        ],
        compiler_params=params(),
        name="student",
    )(emb, smix, target, weight, win, watt, wup, wdown, wout, vecs)


KB = 512


def back_kernel(et_ref, es_ref, stat_ref, smix_ref, dmix_ref, weight_ref, sq_ref, sv_ref, skt_ref, dsum_ref, emb_ref, first_ref,
                wqkv_ref, vgrad_ref, part_in, late_ref, block_ref, part_ref,
                dkv, dqt, ds, dq, dfirst, dmt, dmz, sqd, rows, flat, vecs, kls, sem):
    j, kb = pl.program_id(0), pl.program_id(1)
    s_scale = HEAD_S**-0.5
    late = pltpu.make_async_copy(late_ref, flat.at[896:5632], sem)

    @pl.when((j == 0) & (kb == 0))
    def _():
        late.start()
        dkv[...] = jnp.zeros_like(dkv)
        kls[...] = jnp.zeros_like(kls)

    @pl.when(kb == 0)
    def _():
        quarter = weight_ref[0] * (1.0 / HEADS)
        wide = dmix_ref[...].astype(F32)
        tall = wide.T
        place = lax.broadcasted_iota(jnp.int32, (D_S, 1), 0) // HEAD_S
        for h in range(HEADS):
            own = slice(h * HEAD_S, h * HEAD_S + HEAD_S)
            mine = slice(h * QB, h * QB + QB)
            t_inv, s_inv = stat_ref[0, h, 0:1, :], stat_ref[0, h, 1:2, :]
            kls[0:1, :] += quarter * stat_ref[0, h, 2:3, :]
            row_dot = jnp.sum(tall[own] * smix_ref[0, own, :], 0, keepdims=True)
            rows[h, 0:1, :] = row_dot - quarter
            rows[h, 1:2, :] = s_inv
            rows[h, 2:3, :] = quarter * t_inv
            dmt[h] = jnp.where(place == h, tall, 0.0).astype(BF16)
            dmz[mine, :] = head_lanes(wide * stat_ref[0, h].T[:, 1:2], h).astype(BF16)
            sqd[mine, :] = head_lanes(sq_ref[...], h)
        dqt[...] = jnp.zeros_like(dqt)

    here = pl.ds(pl.multiple_of(slot_of(j) * SEQ + kb * KB, KB), KB)
    dkv[here, D_S:] += dot(es_ref[0], dmz[...])
    for h in range(HEADS):
        lanes = slice(h * QB, h * QB + QB)
        for c in range(KB // 256):
            part = slice(c * 256, c * 256 + 256)
            d_probs = dot(sv_ref[part, :], dmt[h])
            s_exp, t_exp = es_ref[0, part, lanes].astype(F32), et_ref[0, part, lanes].astype(F32)
            d_scores = (d_probs - rows[h, 0:1, :]) * rows[h, 1:2, :] * s_exp - t_exp * rows[h, 2:3, :]
            ds[part, lanes] = d_scores.astype(BF16)
        own = slice(h * HEAD_S, h * HEAD_S + HEAD_S)
        dqt[own, :] += dot(skt_ref[own, :], ds[:, lanes])
    dkv[here, :D_S] += dot(ds[...], sqd[...])

    @pl.when(kb == pl.num_programs(1) - 1)
    def _():
        dq[pl.ds(pl.multiple_of(j * QB, QB), QB), :] = (dqt[...] * s_scale).T

    @pl.when((j == 2) & (kb == pl.num_programs(1) - 1))
    def _():
        qkv_w = wqkv_ref[...]
        dq_low = dq[...].astype(BF16)
        own = pl.ds(pl.multiple_of(first_block() * QB, QB), OWN)
        q_grad = dot_tn(first_ref[own, :], dq_low)
        own_part = dsum_ref[...] + dot_nt(dq_low, qkv_w[:, :D_S])
        kv_grad = jnp.zeros((D_S, 2 * D_S), F32)
        kv_bias = jnp.zeros((1, 2 * D_S), F32)
        for c in range(8):
            part = pl.ds(c * 512, 512)
            wide = dkv[part, :]
            low = jnp.concatenate([(wide[:, :D_S] * s_scale).astype(BF16), wide[:, D_S:].astype(BF16)], 1)
            kv_grad += dot_tn(first_ref[part, :], low)
            kv_bias += jnp.sum(low.astype(F32), 0, keepdims=True)
            dfirst[part, :] = dot_nt(low, qkv_w[:, D_S:])
        dfirst[own, :] += own_part
        in_grad = jnp.zeros((D_S, D_E), F32)
        in_bias = jnp.zeros((1, D_S), F32)
        for c in range(8):
            part = pl.ds(c * 512, 512)
            low = dfirst[part, :].astype(BF16)
            in_grad += dot_tn(low, emb_ref[part, :])
            in_bias += jnp.sum(low.astype(F32), 0, keepdims=True)
        flat[0:512, :] = in_grad.T
        flat[pl.ds(512, 128, stride=3), :] = q_grad
        flat[pl.ds(513, 128, stride=3), :] = kv_grad[:, :D_S]
        flat[pl.ds(514, 128, stride=3), :] = kv_grad[:, D_S:]
        vecs[...] = vgrad_ref[...]
        vecs[0:1, :] = in_bias
        vecs[1:2, :] = jnp.sum(dq_low.astype(F32), 0, keepdims=True)
        vecs[2:3, :] = kv_bias[:, :D_S]
        vecs[3:4, :] = kv_bias[:, D_S:]
        late.wait()
        lane = lax.broadcasted_iota(jnp.int32, (1, 128), 1)
        rest = jnp.zeros((BLOCK - SHARD - 1, 128), F32)
        for pair in range(64):
            both = flat[88 * pair : 88 * pair + 88, :]
            for i in range(2):
                owner = 2 * pair + i
                row, shift = divmod(47 * owner, 128)
                entries = vecs[row : row + 1, :]
                if shift + 47 > 128:
                    entries = jnp.where(lane >= shift, entries, vecs[row + 1 : row + 2, :])
                if shift:
                    entries = pltpu.roll(entries, 128 - shift, 1)
                entries = jnp.where(lane < 47, entries, 0.0)
                mine = both[SHARD * i : SHARD * (i + 1)]
                block_ref[owner // 32, owner // 16 % 2, owner % 16] = jnp.concatenate([mine, entries, rest], 0).astype(BF16)
        kl = jnp.sum(kls[0:1, :], keepdims=True)
        corner = (lax.broadcasted_iota(jnp.int32, (8, 128), 0) == 0) & (lax.broadcasted_iota(jnp.int32, (8, 128), 1) == 0)
        part_ref[...] = part_in[...] + jnp.where(corner, kl, 0.0)


def back(et, es, stat, smix, dmix, weight, sq, sv, skt, dsum, emb, first, wqkv, vgrad, part, late):
    count = SEQ // KB
    place = lambda j, k: slot_of(j) * count + k
    return pl.pallas_call(
        back_kernel,
        grid=(3, count),
        in_specs=[
            pl.BlockSpec((1, KB, HEADS * QB), lambda j, k: (j, k, 0)),
            pl.BlockSpec((1, KB, HEADS * QB), lambda j, k: (j, k, 0)),
            pl.BlockSpec((1, HEADS, 8, QB), lambda j, k: (j, 0, 0, 0)),
            pl.BlockSpec((1, D_S, QB), lambda j, k: (j, 0, 0)),
            pl.BlockSpec((QB, D_S), lambda j, k: (j, 0)),
            pl.BlockSpec((1, 1, QB), lambda j, k: (j, 0, 0)),
            pl.BlockSpec((QB, D_S), lambda j, k: (first_block() + j, 0)),
            pl.BlockSpec((KB, D_S), lambda j, k: (place(j, k), 0)),
            pl.BlockSpec((D_S, KB), lambda j, k: (0, place(j, k))),
            whole(OWN, D_S),
            whole(SLOTS, D_E),
            whole(SLOTS, D_S),
            whole(D_S, 3 * D_S),
            whole(48, 128),
            whole(8, 128),
            pl.BlockSpec(memory_space=pl.ANY),
        ],
        out_specs=[whole(4, 2, 16, BLOCK, 128), whole(8, 128)],
        out_shape=[
            jax.ShapeDtypeStruct((4, 2, 16, BLOCK, 128), BF16),
            jax.ShapeDtypeStruct((8, 128), F32),
        ],
        scratch_shapes=[
            pltpu.VMEM((SLOTS, 2 * D_S), F32),
            pltpu.VMEM((D_S, QB), F32),
            pltpu.VMEM((KB, HEADS * QB), BF16),
            pltpu.VMEM((OWN, D_S), F32),
            pltpu.VMEM((SLOTS, D_S), F32),
            pltpu.VMEM((HEADS, D_S, QB), BF16),
            pltpu.VMEM((HEADS * QB, D_S), BF16),
            pltpu.VMEM((HEADS * QB, D_S), BF16),
            pltpu.VMEM((HEADS, 8, QB), F32),
            pltpu.VMEM((5632, 128), F32),
            pltpu.VMEM((48, 128), F32),
            pltpu.VMEM((8, QB), F32),
            pltpu.SemaphoreType.DMA,
        ],
        compiler_params=params(),
        name="back",
    )(et, es, stat, smix, dmix, weight, sq, sv, skt, dsum, emb, first, wqkv, vgrad, part, late)


def update_kernel(g_ref, part_ref, master_mat, master_vec, first_mat, first_vec, second_mat, second_vec,
                  new_ref, newf_ref, news_ref, scal_ref, packs, half_in, mine, block_out, blocks_in, tile_out, tiles_f, tiles_d,
                  half_sems, block_send, block_recv, f_send, f_recv, d_send, d_recv):
    dp, fs = lax.axis_index("dp"), lax.axis_index("fsdp")
    x, core = dp // 2, dp % 2
    sibling = (2 * x + 1 - core, fs)
    barrier = pltpu.get_barrier_semaphore()

    def chip(k):
        return (2 * ((x + k // 16) % 4) + core, (fs + k) % 16)

    def greet(k, _):
        pl.semaphore_signal(barrier, inc=1, device_id=chip(k), device_id_type=MESH)
        return 0

    lax.fori_loop(1, 64, greet, 0)
    for k in range(4):
        other = (2 * ((x + k) % 4) + 1 - core, fs)
        pl.semaphore_signal(barrier, inc=1, device_id=other, device_id_type=MESH)

    packs[...] = jnp.zeros_like(packs)
    for i, (mat, vec) in enumerate([(master_mat, master_vec), (first_mat, first_vec), (second_mat, second_vec)]):
        packs[i, 0:SHARD, :] = mat[...]
        packs[i, SHARD : SHARD + 1, 0:47] = vec[...]
    pl.semaphore_wait(barrier, 67)
    swap = pltpu.make_async_remote_copy(
        g_ref.at[:, 1 - core], half_in, half_sems.at[0], half_sems.at[1], device_id=sibling, device_id_type=MESH
    )
    swap.start()
    swap.wait()

    def join(i, _):
        summed = g_ref[i // 16, core, i % 16].astype(F32) + half_in[i // 16, i % 16].astype(F32)
        block_out[i] = summed.astype(BF16)
        return 0

    lax.fori_loop(0, 64, join, 0)
    mine[...] = g_ref[x, core, fs].astype(F32) + half_in[x, fs].astype(F32)

    def block_copy(k):
        xk, fk = (x + k // 16) % 4, (fs + k) % 16
        return pltpu.make_async_remote_copy(
            block_out.at[xk * 16 + fk], blocks_in.at[k], block_send.at[k], block_recv.at[k],
            device_id=(2 * xk + core, fk), device_id_type=MESH,
        )

    def start(k, _):
        block_copy(k).start()
        return 0

    lax.fori_loop(1, 64, start, 0)

    def gather(k, _):
        block_copy(k).wait()
        mine[...] += blocks_in[k].astype(F32)
        return 0

    lax.fori_loop(1, 64, gather, 0)

    row = lax.broadcasted_iota(jnp.int32, (BLOCK, 128), 0)
    lane8 = lax.broadcasted_iota(jnp.int32, (8, 128), 1)
    row8 = lax.broadcasted_iota(jnp.int32, (8, 128), 0)
    place = (dp * 16 + fs) * SHARD + row
    is_matrix = row < SHARD
    bounds = [0]
    for rows in MAT_ROWS:
        bounds.append(bounds[-1] + rows)
    members = [is_matrix & (place >= bounds[i]) & (place < bounds[i + 1]) for i in range(6)]

    def everyone(tile, turn):
        tile_out[turn, 0] = tile
        tiles_f[turn, fs] = tile

        def f_copy(k):
            return pltpu.make_async_remote_copy(
                tile_out.at[turn, 0], tiles_f.at[turn, fs], f_send.at[turn, k], f_recv.at[turn, k],
                device_id=(dp, (fs + k) % 16), device_id_type=MESH,
            )

        def d_copy(k):
            return pltpu.make_async_remote_copy(
                tile_out.at[turn, 1], tiles_d.at[turn, dp], d_send.at[turn, k], d_recv.at[turn, k],
                device_id=((dp + k) % 8, fs), device_id_type=MESH,
            )

        for k in range(1, 16):
            f_copy(k).start()
        for k in range(1, 16):
            f_copy(k).wait()
        total = tiles_f[turn, 0]
        for k in range(1, 16):
            total = total + tiles_f[turn, k]
        tile_out[turn, 1] = total
        tiles_d[turn, dp] = total
        for k in range(1, 8):
            d_copy(k).start()
        for k in range(1, 8):
            d_copy(k).wait()
        total = tiles_d[turn, 0]
        for k in range(1, 8):
            total = total + tiles_d[turn, k]
        return total

    def entry(tile, i):
        return jnp.sum(jnp.where((row8 == 0) & (lane8 == i), tile, 0.0), keepdims=True)

    def tile_of(values):
        tile = jnp.zeros((8, 128), F32)
        for i, value in values:
            tile += jnp.where((row8 == 0) & (lane8 == i), value, 0.0)
        return tile

    grad = mine[...]
    master = packs[0]
    squares = master * master
    tile = part_ref[...] + tile_of(
        [(2, jnp.sum(grad * grad, keepdims=True))]
        + [(3 + i, jnp.sum(jnp.where(members[i], squares, 0.0), keepdims=True)) for i in range(6)]
    )
    tile = everyone(tile, 0)
    loss, count = entry(tile, 0), entry(tile, 1)
    inverse = 1.0 / count
    norm = jnp.sqrt(entry(tile, 2)) * inverse
    factor = CLIP_NORM / jnp.maximum(norm, CLIP_NORM)
    grad = grad * inverse * factor
    first = BETA_ONE * packs[1] + (1.0 - BETA_ONE) * grad
    second = BETA_TWO * packs[2] + (1.0 - BETA_TWO) * grad * grad
    newf_ref[...] = first
    news_ref[...] = second
    ratio = first / (1.0 - BETA_ONE**STEP) / (jnp.sqrt(second / (1.0 - BETA_TWO**STEP)) + ADAM_EPS)
    ratio = ratio + jnp.where(is_matrix, WEIGHT_DECAY * master, 0.0)
    squares = ratio * ratio
    steps = everyone(tile_of([(3 + i, jnp.sum(jnp.where(members[i], squares, 0.0), keepdims=True)) for i in range(6)]), 1)
    trust = jnp.ones((BLOCK, 128), F32)
    for i in range(6):
        trust = jnp.where(members[i], jnp.sqrt(entry(tile, 3 + i)) / jnp.sqrt(entry(steps, 3 + i)), trust)
    new_ref[...] = master - LEARN_RATE * (trust * ratio)
    scal_ref[...] = tile_of([(0, loss), (1, count), (2, norm)])


def update(grads, part, *state):
    vmem = pl.BlockSpec(memory_space=pltpu.VMEM)
    block = jax.ShapeDtypeStruct((BLOCK, 128), F32)
    dma = pltpu.SemaphoreType.DMA
    return pl.pallas_call(
        update_kernel,
        in_specs=[vmem] * 8,
        out_specs=[vmem] * 4,
        out_shape=[block, block, block, jax.ShapeDtypeStruct((8, 128), F32)],
        scratch_shapes=[
            pltpu.VMEM((3, BLOCK, 128), F32),
            pltpu.VMEM((4, 16, BLOCK, 128), BF16),
            pltpu.VMEM((BLOCK, 128), F32),
            pltpu.VMEM((64, BLOCK, 128), BF16),
            pltpu.VMEM((64, BLOCK, 128), BF16),
            pltpu.VMEM((2, 2, 8, 128), F32),
            pltpu.VMEM((2, 16, 8, 128), F32),
            pltpu.VMEM((2, 8, 8, 128), F32),
            dma((2,)),
            dma((64,)),
            dma((64,)),
            dma((2, 16)),
            dma((2, 16)),
            dma((2, 8)),
            dma((2, 8)),
        ],
        compiler_params=params(collective_id=1, has_side_effects=True),
        name="update",
    )(grads, part, *state)


def finish_kernel(new_ref, newf_ref, news_ref, scal_ref, loss, count, norm, m0, m1, m2, v0, v1, v2):
    for source, mat, vec in ((new_ref, m0, v0), (newf_ref, m1, v1), (news_ref, m2, v2)):
        mat[...] = source[0:SHARD, :]
        vec[...] = source[SHARD : SHARD + 1, 0:47]
    for i, out in enumerate((loss, count, norm)):
        out[...] = scal_ref[0:1, i : i + 1]


def finish(*made):
    vmem = pl.BlockSpec(memory_space=pltpu.VMEM)
    shape = lambda *dims: jax.ShapeDtypeStruct(dims, F32)
    return pl.pallas_call(
        finish_kernel,
        in_specs=[vmem] * 4,
        out_specs=[vmem] * 9,
        out_shape=[shape(1, 1)] * 3 + [shape(SHARD, 128)] * 3 + [shape(1, 47)] * 3,
        name="finish",
    )(*made)


def per_device(
    token_ids,
    splits,
    valid_mask,
    embed_table,
    embed_proj,
    embed_bias,
    type_table,
    teach_in,
    teach_qkv,
    teach_att,
    teach_up,
    teach_down,
    teach_out,
    teach_bias,
    teach_gain,
    teach_shift,
    matrices,
    vectors,
    matrix_first,
    matrix_second,
    vector_first,
    vector_second,
):
    mat = lambda v: v.reshape(SHARD, 128)
    vec = lambda v: v.reshape(1, 47)
    rows_128 = lambda v: v.reshape(-1, 128)
    bias = rows_128(teach_bias)
    spread_rows, weights, packed = spread(embed_table[token_ids], valid_mask, mat(matrices), vec(vectors))
    (
        emb, t_keys, t_values, first, s_q, s_k, s_v, s_kt, s_vt, own_emb, hidden, t_queries,
        in_w, qkv_w, att_w, up_w, down_w, out_w, vecs,
    ) = project(
        splits, spread_rows.reshape(SLOTS, 128), packed, embed_proj, rows_128(embed_bias), type_table, teach_in, teach_qkv, bias
    )
    et, es, t_mixed, s_mixed, stat = attend(t_queries, t_keys, t_values, s_q, s_k, s_vt)
    target = teacher(
        t_mixed, hidden, own_emb, teach_att, teach_up, teach_down, teach_out, bias, rows_128(teach_gain), rows_128(teach_shift)
    )
    late, vgrads, d_sum, d_mixed, part = student(
        own_emb, s_mixed, target, weights, in_w, att_w, up_w, down_w, out_w, vecs
    )
    blocks, part = back(
        et, es, stat, s_mixed, d_mixed, weights, s_q, s_v, s_kt, d_sum, emb, first, qkv_w, vgrads, part, late
    )
    made = update(
        blocks, part, mat(matrices), vec(vectors), mat(matrix_first), vec(vector_first), mat(matrix_second), vec(vector_second)
    )
    loss, count, norm, m0, m1, m2, v0, v1, v2 = finish(*made)
    flat = lambda v: v.reshape(-1)
    scalar = lambda v: v.reshape(())
    return (
        scalar(loss), scalar(count), scalar(norm), flat(m0), flat(m1), flat(m2), flat(v0), flat(v1), flat(v2),
    )


def solution(mesh):
    both = P(("dp", "fsdp"))
    return jax.shard_map(
        per_device,
        mesh=mesh,
        in_specs=(P("dp", "fsdp"), P("dp"), P("dp", "fsdp")) + (P(),) * 13 + (both,) * 6,
        out_specs=(P(), P(), P(), both, both, both, both, both, both),
        check_vma=False,
    )
```

time: 280 us -> 234 us (0.84)
  local copies, waits for them, and re-layouts: 36.2 us -> 6.5 us
  between operations: 15.6 us -> 0.68 us
  Pallas kernels: 212 us -> 225 us
  other arithmetic: 11.5 us -> 0.7 us
  waiting for transfers between devices: 2.83 us -> 0 us
    pallas_call x7 -> x6, Pallas kernels: 174 us -> 187 us  [the longest x1 46.9 us: update(): pl.pallas_call(update_kernel, in_specs=[vmem] * 8, out_specs=[vmem] * 4,...]
    reshape x14 -> x0, local copies, waits for them, and re-layouts: 12.6 us -> none  [the longest x3 4.04 us: per_device(): mats = lambda v: v[:SHARD].reshape(-1)]
    concatenate x6 -> x0, other arithmetic: 6.97 us -> none  [the longest x1 2.77 us: per_device(): grads = jnp.concatenate([grads_d, grads_c]).reshape(128, SHARD, 128)]
    slice x8 -> x0, local copies, waits for them, and re-layouts: 4.75 us -> none  [the longest x1 1.38 us: per_device(): scalars[0, 2]]
    squeeze x3 -> x0, local copies, waits for them, and re-layouts: 3.57 us -> none  [per_device(): vecs_of = lambda v: v[SHARD, :47]]
    concatenate x5 -> x0, local copies, waits for them, and re-layouts: 3.41 us -> none  [the longest x2 2.67 us: per_device(): jnp.concatenate([grads, jnp.pad(vgrads, ((0, 0), (0, 0), (0, 81))), jnp.z...]
    all_gather x1 -> x0, waiting for transfers between devices: 2.81 us -> none  [per_device(): lax.all_gather(master.astype(BF16), ('dp', 'fsdp'), axis=0, tiled=False)]
  transfers between devices with their start and end apart: 1 -> 0, of which waited for: 1 -> 0; matrix products, arithmetic and copies ran while one was open for 6% -> 0% of each run, Pallas kernels for 21% -> 0%
where the time goes in v2:
time: 234 us; the launch traced here: 233 us
  Pallas kernels  225 us (96%)
  local copies, waits for them, and re-layouts  6.5 us (3%)
    pallas_call x1, Pallas kernels, update(): pl.pallas_call(update_kernel, in_specs=[vmem] * 8, out_specs=[vmem] * 4,...  46.9 us
    pallas_call x1, Pallas kernels, project(): pl.pallas_call(project_kernel, grid=(TILES + 1,), in_specs=[pl.BlockSpec(...  42.5 us
    pallas_call x1, Pallas kernels, spread(): pl.pallas_call(spread_kernel, in_specs=[vmem] * 4, out_specs=[vmem] * 3,...  36.5 us
    pallas_call x1, Pallas kernels, back(): pl.pallas_call(back_kernel, grid=(3, count), in_specs=[pl.BlockSpec((1, K...  32 us
    pallas_call x1, Pallas kernels, attend(): pl.pallas_call(attend_kernel, grid=(STEPS + 1,), in_specs=[pl.BlockSpec((...  28 us
    pallas_call x1, Pallas kernels, teacher(): pl.pallas_call(teacher_kernel, grid=(FF_T // FC,), in_specs=[whole(OWN, D...  25.9 us
    pallas_call x1, Pallas kernels, student(): pl.pallas_call(student_kernel, grid=(1,), in_specs=[whole(OWN, D_E), whol...  12.3 us
    gather x1, local copies, waits for them, and re-layouts, per_device(): embed_table[token_ids]  6.5 us

profile of v2, /device:TPU:1, one launch (start us, length us, event | category | flops | bytes accessed | tf_op | source)
XLA Modules:
  0.0 233.4 jit_solution(4609719964582765764)
XLA Ops:
  0.6 0.7 fusion
  1.3 6.5 %gather_fusion = bf16[768,128]{1,0:T(8,128)(2,1)} fusion(bf16[30522,128]{1,0:T(8,128)(2,1)} %param.25, s32[1024]{0:T(1024)S(1)} %pad_clamp_fusion), kind=kCustom, calls=%fused_computation | custom fusion | bytes 396288 | tf_op jit(solution)/shard_map/gather | solution.py:1027
  7.8 36.5 %spread.1 = (bf16[2,16,128,128]{3,2,1,0:T(8,128)(2,1)}, f32[3,1,256]{2,1,0:T(1,128)}, bf16[128,48,128]{2,1,0:T(8,128)(2,1)}) custom-call(bf16[6,128,128]{2,1,0:T(8,128)(2,1)} %bitcast.24, s32[6,128]{1,0:T(8,128)} %mask_in.1, f32[44,128]{1,0:T(8,128)} %bitcast.27, f32[1,47]{1,0:T(1,128)} %bitcast.34), custom_call_target="tpu_custom_call" | custom-call | tf_op jit(solution)/shard_map/spread/pallas_call | solution.py:226
  44.4 42.5 %project.1 = (bf16[4096,512]{1,0:T(8,128)(2,1)}, bf16[4096,1024]{1,0:T(8,128)(2,1)}, bf16[1024,4096]{1,0:T(8,128)(2,1)}, bf16[4096,128]{1,0:T(8,128)(2,1)}, bf16...) custom-call(s32[6]{0:T(128)} %splits_ref.1, ...), custom_call_target="tpu_custom_call" | custom-call | tf_op jit(solution)/shard_map/project/pallas_call | solution.py:354
  86.9 28.0 %attend.1 = (bf16[3,2048,1024]{2,1,0:T(8,128)(2,1)}, bf16[3,2048,1024]{2,1,0:T(8,128)(2,1)}, bf16[768,1024]{1,0:T(8,128)(2,1)}, f32[3,128,256]{2,1,0:T(8,128)}, f32[3,4,8,256]{3,2,1,0:T(8,128)}) custom-call(bf16[768,1024]{1,0:T(8,128)(2,1)} %get-tuple-element.58.tq_ref, bf16[4096,1024]{1,0:T(8,128)(2,1)} %get-tuple-element.59.tk_ref, ...), custom_call_target="tpu_custom_call" | custom-call | tf_op jit(solution)/shard_map/attend/pallas_call | solution.py:459
  114.9 25.9 %teacher.1.target_ref = f32[768,512]{1,0:T(8,128)} custom-call(bf16[768,1024]{1,0:T(8,128)(2,1)} %get-tuple-element.69.mix_ref, f32[768,1024]{1,0:T(8,128)} %get-tuple-element.70.hid_ref, bf16[768,512]{1,0:T(8,128)(2,1)} %get-tuple-element.68.emb_ref, bf16[1024,1024]{1,0:T(8,128)(2,1)} %att_ref.1, bf16[1024,4096]{1,0:T(8,128)(2,1)} %up_ref.1, ...), custom_call_target="tpu_custom_call" | custom-call | tf_op jit(solution)/shard_map/teacher/pallas_call | solution.py:525
  140.7 12.3 %student.1 = (f32[4736,128]{1,0:T(8,128)}, f32[48,128]{1,0:T(8,128)}, f32[768,128]{1,0:T(8,128)}, bf16[768,128]{1,0:T(8,128)(2,1)}, f32[8,128]{1,0:T(8,128)}) custom-call(bf16[768,512]{1,0:T(8,128)(2,1)} %get-tuple-element.68.emb_ref, f32[3,128,256]{2,1,0:T(8,128)} %get-tuple-element.67.smix_ref, f32[768,512]{1,0:T(8,128)} %teacher.1.target_ref, ...), custom_call_target="tpu_custom_call" | custom-call | tf_op jit(solution)/shard_map/student/pallas_call | solution.py:618
  153.0 32.0 %back.1 = (bf16[4,2,16,48,128]{4,3,2,1,0:T(8,128)(2,1)}, f32[8,128]{1,0:T(8,128)}) custom-call(bf16[3,2048,1024]{2,1,0:T(8,128)(2,1)} %get-tuple-element.64.et_ref, bf16[3,2048,1024]{2,1,0:T(8,128)(2,1)} %get-tuple-element.65.es_ref, f32[3,4,8,256]{3,2,1,0:T(8,128)} %get-tuple-element.66.stat_ref, f32[3,128,256]{2,1,0:T(8,128)} %get-tuple-element.67.smix_ref, ...), custom_call_target="tpu_custom_call" | custom-call | tf_op jit(solution)/shard_map/back/pallas_call | solution.py:762
  185.1 46.9 %update.1 = (f32[48,128]{1,0:T(8,128)}, f32[48,128]{1,0:T(8,128)}, f32[48,128]{1,0:T(8,128)}, f32[8,128]{1,0:T(8,128)}) custom-call(bf16[4,2,16,48,128]{4,3,2,1,0:T(8,128)(2,1)} %get-tuple-element.88.g_ref, f32[8,128]{1,0:T(8,128)} %get-tuple-element.89.part_ref, f32[44,128]{1,0:T(8,128)} %bitcast.28, f32[1,47]{1,0:T(1,128)} %bitcast.35, ...), custom_call_target="tpu_custom_call" | custom-call | tf_op jit(solution)/shard_map/update/pallas_call | solution.py:952
  231.9 1.4 finish.1
  (1 shorter events, 0.0 us)
